TPU v7x, 256 devices: a whole 4x4x8 slice. The times are simulated.
256 devices in a mesh: group: 8 (over x, core), head: 32 (over y, z).
Axes of the slice: x: 4, y: 4, z: 8, core: 2. Of those that a mesh axis runs over, the one named last changes fastest.
Arguments:
- query_latent: bfloat16 [2048, 1536], P(('group', 'head')), may hold values from -6 to 6
- response_keys: bfloat16 [2048, 576], P(('group', 'head')), may hold values from -8 to 8
- prompt_cache: bfloat16 [256, 147456], P(('group', 'head')), may hold values from -1376 to 1376
- owners: int32 [8], P('group'), may hold values from 0 to 31, as said below
- lengths: int32 [8, 16], P('group'), may hold values from 1 to 16
- w_query_plain: bfloat16 [1536, 16384], P('group', 'head'), may hold values from -0.15625 to 0.15625
- w_query_rotary: bfloat16 [1536, 8192], P('group', 'head'), may hold values from -0.15625 to 0.15625
- w_key_up: bfloat16 [16384, 512], P('head'), may hold values from -0.5 to 0.5
- w_value_up: bfloat16 [512, 16384], P(None, 'head'), may hold values from -0.5 to 0.5
Outputs:
- head_mix: bfloat16 [2048, 16384], P(('group', 'head'))
Inputs may be any that keep to these rules, and one draw needn't show every extreme that they name: The 1 group whose tokens lie on one index of group have distinct owners. `lengths`: A response's live tokens are its first ones.
All inputs are finite; a program needn't handle non-finite values.
Results may differ from a plain program's by a relative error of at most 0.024.
Values may be sent and summed in bfloat16 or wider, within the bound.
A program may use at most 192 MiB of HBM per device.

v0:
```python
import math

import jax
import jax.numpy as jnp
from jax import lax
from jax.sharding import PartitionSpec as P

LAT = 512
ROPE = 64
NOPE = 128
VDIM = 128
PLEN = 256
RESP = 16
RTOK = 16


def broadcast(value, axis, source):
    kept = jnp.where(lax.axis_index(axis) == source, value, 0).astype(value.dtype)
    return lax.psum(kept, axis)


def rotate(values, first_position, period):
    row_count = values.shape[0]
    half_width = values.shape[-1] // 2
    position = (first_position + jnp.arange(row_count) % period).astype(jnp.float32)
    inverse = jnp.exp(
        jnp.arange(half_width).astype(jnp.float32) * (-2.0 * math.log(10000.0) / values.shape[-1])
    )
    angle = position[:, None, None] * inverse[None, None, :]
    cosine = jnp.cos(angle)
    sine = jnp.sin(angle)
    former = values[..., :half_width]
    latter = values[..., half_width:]
    return jnp.concatenate(
        [former * cosine - latter * sine, latter * cosine + former * sine], axis=-1
    )


def attend(prompt_scores, own_scores, allowed, latent, fresh_latent, value_up, live):
    own_masked = jnp.where(allowed[:, None, :], own_scores, -jnp.inf)
    row_top = jnp.maximum(jnp.max(prompt_scores, axis=0), jnp.max(own_masked, axis=0))
    prompt_exp = jnp.exp(prompt_scores - row_top)
    own_exp = jnp.exp(own_masked - row_top)
    denominator = jnp.sum(prompt_exp, axis=0) + jnp.sum(own_exp, axis=0)
    prompt_weight = (prompt_exp / denominator).astype(jnp.bfloat16)
    own_weight = (own_exp / denominator).astype(jnp.bfloat16)
    mixed = jnp.einsum("pht,pl->htl", prompt_weight, latent, preferred_element_type=jnp.float32)
    mixed = mixed + jnp.einsum(
        "sht,sl->htl", own_weight, fresh_latent, preferred_element_type=jnp.float32
    )
    mixed = mixed.astype(jnp.bfloat16)
    output = jnp.einsum("htl,lhv->thv", mixed, value_up, preferred_element_type=jnp.float32)
    output = output.reshape(output.shape[0], output.shape[1] * output.shape[2])
    return jnp.where(live[:, None], output, 0.0).astype(jnp.bfloat16)


def local(
    query_latent,
    response_keys,
    prompt_cache,
    owners,
    lengths,
    w_query_plain,
    w_query_rotary,
    w_key_up,
    w_value_up,
):
    row_latent, row_keys = (
        lax.all_gather(query_latent, "head", axis=0, tiled=True),
        lax.all_gather(response_keys, "head", axis=0, tiled=True),
    )
    row_count = row_latent.shape[0]
    head_count = w_key_up.shape[0] // NOPE
    group_tokens = RESP * RTOK
    scale_factor = 1.0 / math.sqrt(NOPE + ROPE)
    plain_sum = jnp.dot(
        row_latent,
        lax.all_gather(w_query_plain, "group", axis=0, tiled=True),
        preferred_element_type=jnp.float32,
    )
    rotary_sum = jnp.dot(
        row_latent,
        lax.all_gather(w_query_rotary, "group", axis=0, tiled=True),
        preferred_element_type=jnp.float32,
    )
    plain = plain_sum.astype(jnp.bfloat16).reshape(row_count, head_count, NOPE)
    turned = rotate(rotary_sum.reshape(row_count, head_count, ROPE), PLEN, RTOK).astype(
        jnp.bfloat16
    )
    absorbed = jnp.einsum(
        "thn,hnl->htl",
        plain,
        w_key_up.reshape(head_count, NOPE, LAT),
        preferred_element_type=jnp.float32,
    ).astype(jnp.bfloat16)
    value_up = w_value_up.reshape(LAT, head_count, VDIM)
    places = jnp.arange(group_tokens)
    within = places % RTOK
    response_of = places // RTOK
    allowed = (response_of[:, None] == response_of[None, :]) & (within[:, None] <= within[None, :])
    cached = broadcast(prompt_cache, "head", owners[0]).reshape(-1)
    latent = cached[: PLEN * LAT].reshape(PLEN, LAT)
    rotary = cached[PLEN * LAT :].reshape(ROPE, PLEN)
    prompt_scores = jnp.einsum("htl,pl->pht", absorbed, latent, preferred_element_type=jnp.float32)
    prompt_scores = prompt_scores + jnp.einsum(
        "thr,rp->pht", turned, rotary, preferred_element_type=jnp.float32
    )
    prompt_scores = prompt_scores * scale_factor
    own_scores = jnp.einsum(
        "htl,sl->sht", absorbed, row_keys[:, :LAT], preferred_element_type=jnp.float32
    )
    own_scores = own_scores + jnp.einsum(
        "thr,sr->sht", turned, row_keys[:, LAT:], preferred_element_type=jnp.float32
    )
    own_scores = own_scores * scale_factor
    live = (jnp.arange(RTOK)[None, :] < lengths[0][:, None]).reshape(group_tokens)
    outputs = attend(prompt_scores, own_scores, allowed, latent, row_keys[:, :LAT], value_up, live)
    return lax.all_to_all(outputs, "head", split_axis=0, concat_axis=1, tiled=True)


def solution(mesh):
    return jax.shard_map(
        local,
        mesh=mesh,
        in_specs=(
            P(("group", "head"), None),
            P(("group", "head"), None),
            P(("group", "head"), None),
            P("group"),
            P("group", None),
            P("group", "head"),
            P("group", "head"),
            P("head", None),
            P(None, "head"),
        ),
        out_specs=P(("group", "head"), None),
        check_vma=False,
    )
```

profile of v0, /device:TPU:2, one launch (start us, length us, event | category | flops | bytes accessed | tf_op | source)
XLA Modules:
  0.0 199.8 jit_solution(6079976928029017855)
XLA Ops:
  8.1 1.4 broadcast_select_fusion
  9.5 0.0 all-gather.2.cloned.1.call-start
  9.6 0.5 all-gather.2.cloned.1.call-update
  10.1 0.1 lt.42
  10.2 0.7 lt.44
  10.9 0.1 lt.45
  11.0 53.8 %all_gather.15 = bf16[256,576]{1,0:T(8,128)(2,1)S(1)} all-gather(bf16[8,576]{1,0:T(8,128)(2,1)} %param.10), channel_id=1, replica_groups=mesh['group'=8,'head'=32] {'head'}, dimensions={0}, use_global_device_ids=true | all-gather | bytes 304128 | tf_op jit(solution)/shard_map/all_gather | solution.py:70
  64.8 47.7 %all_gather.12 = bf16[256,1536]{1,0:T(8,128)(2,1)S(1)} all-gather(bf16[8,1536]{1,0:T(8,128)(2,1)S(1)} %copy-done.2), channel_id=1, replica_groups=mesh['group'=8,'head'=32] {'head'}, dimensions={0}, use_global_device_ids=true | all-gather | bytes 811008 | tf_op jit(solution)/shard_map/all_gather | solution.py:69
  112.6 0.1 broadcast_compare_fusion
  112.6 0.2 multiply_cosine_fusion
  112.8 0.1 compare_and_fusion
  113.0 13.5 %all_gather.14 = bf16[1536,256]{1,0:T(8,128)(2,1)S(1)} all-gather(bf16[192,256]{1,0:T(8,128)(2,1)S(1)} %copy-done.1), channel_id=1, replica_groups=mesh['group'=8,'head'=32] {'group'}, dimensions={0}, use_global_device_ids=true | all-gather | bytes 884736 | tf_op jit(solution)/shard_map/all_gather | solution.py:83
  126.5 0.4 fusion.27
  127.0 35.2 %all-reduce.2.cloned.1.call-done = bf16[1,147456]{1,0:T(2,128)(2,1)} async-done(((bf16[1,147456]{1,0:T(2,128)(2,1)}), bf16[1,147456]{1,0:T(2,128)(2,1)}) %all-reduce.2.cloned.1.call-update) | async-done | bytes 294928 | tf_op jit(solution)/shard_map/psum | solution.py:19
  162.3 2.6 %slice_reduce_fusion = bf16[131072]{0:T(1024)(128)(2,1)S(1)} fusion(bf16[1,147456]{1,0:T(2,128)(2,1)} %all-reduce.2.cloned.1.call-done), kind=kLoop, calls=%fused_computation.24 | loop fusion | bytes 524288 | tf_op jit(solution)/shard_map/slice | solution.py:102
  164.8 0.2 reshape.233
  165.0 1.0 slice_reduce_fusion.1
  166.1 0.0 all-gather.2.cloned.1.call-done
  166.1 2.0 fusion.7
  168.1 0.4 convolution_convert_fusion
  168.5 0.5 convolution_bitcast_fusion.1
  169.0 0.5 fusion.26
  169.5 0.3 fusion.25
  169.8 0.3 fusion.24
  170.1 0.3 fusion.9
  170.5 1.8 fusion.10
  172.3 2.4 %fusion.6 = bf16[256,4,128]{2,0,1:T(8,128)(2,1)S(1)} fusion(f32[4,256,512]{2,1,0:T(8,128)} %fusion.10, f32[256,4,256]{2,0,1:T(8,128)S(1)} %get-tuple-element.14, f32[4,256]{1,0:T(4,128)S(1)} %add.80, f32[4,256]{1,0:T(4,128)S(1)} %max.7, bf16[256,576]{1,0:T(8,128)(2,1)S(1)} %all_gather.15, bf16[512,512]{1,0:T(8,128)(2,1)S(1)} %copy-done.3), kind=kOutput, calls=%fused_computation.11 | convolution fusion | flops 404488192 | bytes 4202496 | tf_op jit(solution)/shard_map/htl,lhv->thv/dot_general | solution.py:52
  174.7 0.2 copy.16
  174.9 0.1 reshape.232
  175.0 0.1 select_convert_fusion
  175.1 16.5 %all_to_all.16 = bf16[32,8,512]{2,1,0:T(8,128)(2,1)S(1)} all-to-all(bf16[32,8,512]{2,1,0:T(8,128)(2,1)S(1)} %select_convert_fusion), channel_id=1, replica_groups=mesh['group'=8,'head'=32] {'head'}, dimensions={0} | all-to-all | bytes 524288 | tf_op jit(solution)/shard_map/all_to_all | solution.py:118
  191.7 0.7 copy.32
  (18 shorter events, 0.1 us)
Async XLA Ops:
  7.4 160.7 %copy-start = (bf16[512,512]{1,0:T(8,128)(2,1)S(1)}, bf16[512,512]{1,0:T(8,128)(2,1)}, u32[]{:S(2)}) copy-start(bf16[512,512]{1,0:T(8,128)(2,1)} %param.16) | copy-start | bytes 1572868
  7.4 57.5 %copy-start.2 = (bf16[8,1536]{1,0:T(8,128)(2,1)S(1)}, bf16[8,1536]{1,0:T(8,128)(2,1)}, u32[]{:S(2)}) copy-start(bf16[8,1536]{1,0:T(8,128)(2,1)} %param.9) | copy-start | bytes 73732
  7.4 105.6 %copy-start.1 = (bf16[192,256]{1,0:T(8,128)(2,1)S(1)}, bf16[192,256]{1,0:T(8,128)(2,1)}, u32[]{:S(2)}) copy-start(bf16[192,256]{1,0:T(8,128)(2,1)} %param.15) | copy-start | bytes 294916
  7.4 154.9 %all-reduce.2.cloned.1.call-start = ((), (), s32[]{:S(2)}) async-start(), calls=%async_computation.1 | async-start | bytes 1179648 | tf_op jit(solution)/shard_map/psum | solution.py:19
  9.5 156.5 %all-gather.2.cloned.1.call-start = ((), (), s32[]{:S(2)}) async-start(), calls=%async_computation.2 | async-start | bytes 1769472 | tf_op jit(solution)/shard_map/all_gather | solution.py:78
  170.4 1.9 copy-start.3
Sparse Core Ops, SparseCore 0:
  11.6 150.6 all-reduce.1
Sparse Core Ops, SparseCore 1:
  12.0 28.1 all-gather.1
where the time goes:
time: 200 us
  blocking collectives  132 us (66%)
  waiting for transfers between devices  35.8 us (18%)
  between operations  15.7 us (8%)
  matrix products  8.66 us (4%)
  local copies, waits for them, and re-layouts  5.69 us (3%)
  other arithmetic  2.31 us (1%)
    all_gather x1, blocking collectives, local(): lax.all_gather(response_keys, 'head', axis=0, tiled=True)  53.8 us
    all_gather x1, blocking collectives, local(): lax.all_gather(query_latent, 'head', axis=0, tiled=True)  47.7 us
    psum x1, waiting for transfers between devices, broadcast(): return lax.psum(kept, axis)  35.2 us
    all_to_all x1, blocking collectives, local(): lax.all_to_all(outputs, 'head', split_axis=0, concat_axis=1, tiled=True)  16.5 us
    all_gather x1, blocking collectives, local(): lax.all_gather(w_query_rotary, 'group', axis=0, tiled=True)  13.5 us
  transfers between devices with their start and end apart: 2, of which 1 were waited for; matrix products, arithmetic and copies ran while one was open for 3% of the time, Pallas kernels for 0%

commit v1 on v0

v1 whole, which is shorter than its diff:
```python
import math

import jax
import jax.numpy as jnp
import numpy as np
from jax import lax
from jax.experimental import pallas as pl
from jax.experimental.pallas import tpu as pltpu
from jax.sharding import PartitionSpec as P

MESH = pl.DeviceIdType.MESH
LAT = 512
ROPE = 64
NOPE = 128
VDIM = 128
QLAT = 1536
PLEN = 256
RTOK = 16
TOK = 256
NX, NY, NZ = 4, 4, 8
SHARD = 192
BF = jnp.bfloat16
F32 = jnp.float32
SCALE = 1.0 / math.sqrt(NOPE + ROPE)
LOG2E = 1.4426950408889634


def rotary_tables():
    position = (PLEN + np.arange(TOK) % RTOK).astype(np.float32)
    inverse = np.exp(np.arange(32).astype(np.float32) * np.float32(-2.0 * math.log(10000.0) / ROPE))
    angle = (position[:, None] * inverse[None, :].astype(np.float32)).astype(np.float32)
    cosine, sine = np.cos(angle), np.sin(angle)
    cos_table = np.tile(np.concatenate([cosine, cosine], 1), (1, 4))
    sin_table = np.tile(np.concatenate([-sine, sine], 1), (1, 4))
    return cos_table.astype(np.float32), sin_table.astype(np.float32)


def dot_nt(a, b):
    return lax.dot_general(a, b, (((1,), (1,)), ((), ())), preferred_element_type=F32)


def kernel(
    owner_ref, query_ref, keys_ref, length_ref, cos_ref, sin_ref,
    prompt_hbm, wp_hbm, wr_hbm, ku_hbm, vu_hbm,
    out_ref,
    wp, wr, ku, vu, flat, stage, q_send, k_send, qb, kb,
    p_send, r_send, p_recv, r_recv, z_send, z_recv, pl_buf,
    x_buf, fresh, fresh_rot, latent, rotary, plain, turned, absorbed, o_send,
    local_sem, wx_send, wx_recv, wc_send, wc_recv,
    qz_send, qz_recv, qy_send, qy_recv, ky_send, ky_recv, kz_send, kz_recv,
    pa_send, pa_recv, pz_send, pz_recv, pg_send, pg_recv, py_send, py_recv,
    o_ssem, o_rsem,
):
    g = lax.axis_index("group")
    h = lax.axis_index("head")
    x, c = g // 2, g % 2
    y, z = h // NZ, h % NZ

    def at_x(d):
        return (lax.rem(x + d, NX) * 2 + c, h)

    def at_y(d):
        return (g, lax.rem(y + d, NY) * NZ + z)

    def at_z(d):
        return (g, y * NZ + lax.rem(z + d, NZ))

    sibling = (x * 2 + 1 - c, h)

    def remote(src, dst, ssem, rsem, device):
        return pltpu.make_async_remote_copy(src, dst, ssem, rsem, device_id=device, device_id_type=MESH)

    barrier = pltpu.get_barrier_semaphore()
    peers = [sibling] + [at_x(d) for d in (1, 2, 3)] + [at_y(d) for d in (1, 2, 3)] + [at_z(d) for d in range(1, 8)]
    for peer in peers:
        pl.semaphore_signal(barrier, inc=1, device_id=peer, device_id_type=MESH)

    mine = pl.ds(pl.multiple_of(g * SHARD, 64), SHARD)
    flat_copy = pltpu.make_async_copy(prompt_hbm, flat, local_sem.at[0])
    flat_copy.start()
    ku_copy = pltpu.make_async_copy(ku_hbm, ku, local_sem.at[1])
    vu_copy = pltpu.make_async_copy(vu_hbm, vu, local_sem.at[2])
    wp_copy = pltpu.make_async_copy(wp_hbm, wp.at[mine], local_sem.at[3])
    wr_copy = pltpu.make_async_copy(wr_hbm, wr.at[mine], local_sem.at[4])
    for copy in (wp_copy, wr_copy, ku_copy, vu_copy):
        copy.start()

    query = query_ref[...].astype(F32)
    packed = jnp.concatenate([query[:, :768], query[:, 768:]], axis=0).astype(BF)
    q_send[...] = packed
    qb[pl.ds(h, 1)] = packed[None]
    keys = keys_ref[...].astype(F32)
    tail = jnp.concatenate([keys[:, 512:], jnp.zeros((8, 64), F32)], axis=1)
    packed = jnp.concatenate(
        [
            jnp.concatenate([keys[:, :256], tail], axis=1),
            jnp.concatenate([keys[:, 256:512], jnp.zeros((8, 128), F32)], axis=1),
        ],
        axis=0,
    ).astype(BF)
    k_send[...] = packed
    kb[pl.ds(y, 1), pl.ds(z, 1)] = packed[None, None]

    pl.semaphore_wait(barrier, len(peers))

    w_out = []
    for d in (1, 3, 2):
        w_out.append(remote(wp_hbm, wp.at[mine], wx_send.at[d, 0], wx_recv.at[d, 0], at_x(d)))
        w_out.append(remote(wr_hbm, wr.at[mine], wx_send.at[d, 1], wx_recv.at[d, 1], at_x(d)))
    w_out.append(remote(wp_hbm, wp.at[mine], wc_send.at[0, 0], wc_recv.at[0, 0], sibling))
    w_out.append(remote(wr_hbm, wr.at[mine], wc_send.at[0, 1], wc_recv.at[0, 1], sibling))
    k_out = [remote(k_send, kb.at[y, z], ky_send.at[d], ky_recv.at[d], at_y(d)) for d in (1, 3, 2)]
    q_out = [remote(q_send, qb.at[h], qz_send.at[d], qz_recv.at[d], at_z(d)) for d in (4, 3, 5, 2, 6, 1, 7)]
    for copy in k_out + q_out + w_out:
        copy.start()

    flat_copy.wait()

    @pl.loop(0, PLEN // 8)
    def _(block):
        for r in range(8):
            row = flat[0:1, pl.ds(pl.multiple_of(block * 4096 + r * 512, 512), 512)].astype(F32)
            stage[pl.ds(block * 8 + r, 1), :] = row
        both = stage[pl.ds(pl.multiple_of(block * 8, 8), 8), :]
        p_send[pl.ds(block // 8, 1), pl.ds(block % 8, 1)] = jnp.concatenate(
            [both[:, :256], both[:, 256:]], axis=0
        ).astype(BF)[None, None]

    @pl.loop(0, NY)
    def _(j):
        for r in range(16):
            row = flat[0:1, pl.ds(pl.multiple_of(PLEN * LAT + j * 4096 + r * 256, 256), 256)].astype(F32)
            stage[pl.ds(r, 1), 0:256] = row
        both = stage[0:16, 0:256].astype(BF)
        r_send[pl.ds(j, 1), 0:1] = both[None, None, :, :128]
        r_send[pl.ds(j, 1), 1:2] = both[None, None, :, 128:]

    p_out = []
    for d in (1, 3, 2):
        there = lax.rem(y + d, NY)
        p_out.append(remote(p_send.at[there], p_recv.at[y], pa_send.at[d, 0], pa_recv.at[d, 0], at_y(d)))
        p_out.append(remote(r_send.at[there], r_recv.at[y], pa_send.at[d, 1], pa_recv.at[d, 1], at_y(d)))
    for copy in p_out:
        copy.start()
    p_recv[pl.ds(y, 1)] = p_send[pl.ds(y, 1)]
    r_recv[pl.ds(y, 1)] = r_send[pl.ds(y, 1)]

    for copy in k_out:
        copy.wait_recv()
    kz_out = [remote(kb.at[:, z], kb.at[:, z], kz_send.at[d], kz_recv.at[d], at_z(d)) for d in (4, 3, 5, 2, 6, 1, 7)]

    for copy in q_out:
        copy.wait_recv()
    row = pl.ds(pl.multiple_of(y * NZ, NZ), NZ)
    qy_out = [remote(qb.at[row], qb.at[row], qy_send.at[d], qy_recv.at[d], at_y(d)) for d in (1, 3, 2)]
    for copy in qy_out + kz_out:
        copy.start()

    owner = owner_ref[0]
    for copy in p_out:
        copy.wait_recv()
    chosen = p_recv[owner // NZ]
    chosen_rot = r_recv[owner // NZ]
    for k in range(NZ):
        z_send[k] = jnp.concatenate([chosen[k], chosen_rot[k % 2]], axis=1)
    pz_out = []
    for d in (4, 3, 5, 2, 6, 1, 7):
        pz_out.append(remote(z_send.at[lax.rem(z + d, NZ)], z_recv.at[z], pz_send.at[d], pz_recv.at[d], at_z(d)))
    for copy in pz_out:
        copy.start()
    z_recv[pl.ds(z, 1)] = z_send[pl.ds(z, 1)]

    wc_out = []

    def pass_on(d):
        there = pl.ds(pl.multiple_of((lax.rem(x + NX - d, NX) * 2 + c) * SHARD, 64), SHARD)
        for i, ref in enumerate((wp, wr)):
            pltpu.make_async_remote_copy(
                ref.at[there], ref.at[there], wx_send.at[d, i], wx_recv.at[d, i], device_id=at_x(d), device_id_type=MESH
            ).wait_recv()
            wc_out.append(remote(ref.at[there], ref.at[there], wc_send.at[d, i], wc_recv.at[d, i], sibling))
            wc_out[-1].start()

    pass_on(1)
    pass_on(3)

    for copy in pz_out:
        copy.wait_recv()
    pl_buf[pl.ds(y, 1), pl.ds(z, 1)] = z_recv[owner % NZ][None, None]
    pg_out = [remote(pl_buf.at[y, z], pl_buf.at[y, z], pg_send.at[d], pg_recv.at[d], at_z(d)) for d in (4, 3, 5, 2, 6, 1, 7)]
    for copy in pg_out:
        copy.start()
    pass_on(2)
    for copy in pg_out:
        copy.wait_recv()
    py_out = []
    for d in (1, 3, 2):
        part = pl_buf.at[y, :, :, 0:256]
        py_out.append(remote(part, part, py_send.at[d, 0], py_recv.at[d, 0], at_y(d)))
        part = pl_buf.at[y, 0:2, :, 256:384]
        py_out.append(remote(part, part, py_send.at[d, 1], py_recv.at[d, 1], at_y(d)))
    for copy in py_out:
        copy.start()

    for copy in qy_out:
        copy.wait_recv()
    gathered = qb[...].astype(F32)
    x_buf[:, :768] = gathered[:, :8].reshape(TOK, 768).astype(BF)
    x_buf[:, 768:] = gathered[:, 8:].reshape(TOK, 768).astype(BF)
    wp_copy.wait()
    wr_copy.wait()
    for d in range(NX):
        there = pl.ds(pl.multiple_of((lax.rem(x + NX - d, NX) * 2 + 1 - c) * SHARD, 64), SHARD)
        for i, ref in enumerate((wp, wr)):
            remote(ref.at[there], ref.at[there], wc_send.at[d, i], wc_recv.at[d, i], sibling).wait_recv()
    rows = x_buf[...]
    plain[...] = jnp.dot(rows, wp[...], preferred_element_type=F32).astype(BF)
    spun = jnp.dot(rows, wr[...], preferred_element_type=F32)
    lane = lax.broadcasted_iota(jnp.int32, (TOK, 256), 1)
    swapped = jnp.where(lane % 64 < 32, pltpu.roll(spun, 224, 1), pltpu.roll(spun, 32, 1))
    turned[...] = (spun * cos_ref[...] + swapped * sin_ref[...]).astype(BF)

    ku_copy.wait()
    for i in range(4):
        absorbed[i] = jnp.dot(
            plain[:, i * 128 : (i + 1) * 128], ku[i * 128 : (i + 1) * 128, :], preferred_element_type=F32
        ).astype(BF)

    for copy in kz_out:
        copy.wait_recv()
    gathered = kb[...].astype(F32).reshape(32, 16, 384)
    fresh[:, :256] = gathered[:, :8, :256].reshape(TOK, 256).astype(BF)
    fresh[:, 256:] = gathered[:, 8:, :256].reshape(TOK, 256).astype(BF)
    rot = gathered[:, :8, 256:].reshape(TOK, 128)
    fresh_rot[...] = (rot + pltpu.roll(rot, 64, 1)).astype(BF)

    lengths = jnp.broadcast_to(length_ref[...], (TOK, 16))
    token = lax.broadcasted_iota(jnp.int32, (TOK, 16), 0)
    slot = lax.broadcasted_iota(jnp.int32, (TOK, 16), 1)
    limit = jnp.sum(jnp.where(token // RTOK == slot, lengths, 0).astype(F32), axis=1, keepdims=True)
    place = (lax.broadcasted_iota(jnp.int32, (TOK, 1), 0) % RTOK).astype(F32)
    live = place < limit

    t_half = lax.broadcasted_iota(jnp.int32, (128, 128), 0)
    s_half = lax.broadcasted_iota(jnp.int32, (128, 128), 1)
    allowed = (t_half // RTOK == s_half // RTOK) & (s_half <= t_half)
    pair_lane = lax.broadcasted_iota(jnp.int32, (TOK, 128), 1)

    for copy in py_out:
        copy.wait_recv()
    gathered = pl_buf[:, :, :, :256].astype(F32).reshape(32, 16, 256)
    latent[:, :256] = gathered[:, :8].reshape(PLEN, 256).astype(BF)
    latent[:, 256:] = gathered[:, 8:].reshape(PLEN, 256).astype(BF)
    for j in range(NY):
        both = jnp.concatenate([pl_buf[j, 0, :, 256:], pl_buf[j, 1, :, 256:]], axis=1)
        rotary[j * 16 : (j + 1) * 16, :] = both
        rotary[64 + j * 16 : 64 + (j + 1) * 16, :] = both
    vu_copy.wait()

    for pair in range(2):
        outs = []
        pair_turned = turned[:, pair * 128 : (pair + 1) * 128]
        for sub in range(2):
            i = pair * 2 + sub
            a = absorbed[i]
            mine_lanes = (pair_lane < 64) if sub == 0 else (pair_lane >= 64)
            t = jnp.where(mine_lanes, pair_turned.astype(F32), 0.0).astype(BF)
            prompt_scores = dot_nt(a, latent[...]) + jnp.dot(t, rotary[...], preferred_element_type=F32)
            own = []
            for half in range(2):
                part = slice(half * 128, (half + 1) * 128)
                scores = dot_nt(a[part], fresh[part, :]) + dot_nt(t[part], fresh_rot[part, :])
                own.append(jnp.where(allowed, scores, -jnp.inf))
            own_scores = jnp.concatenate(own, axis=0)
            top = jnp.max(
                jnp.maximum(jnp.maximum(prompt_scores[:, :128], prompt_scores[:, 128:]), own_scores),
                axis=1,
                keepdims=True,
            )
            prompt_exp = jnp.exp2((prompt_scores - top) * (SCALE * LOG2E))
            own_exp = jnp.exp2((own_scores - top) * (SCALE * LOG2E))
            total = jnp.sum(prompt_exp[:, :128] + prompt_exp[:, 128:] + own_exp, axis=1, keepdims=True)
            factor = jnp.where(live, 1.0 / total, 0.0)
            own_weight = own_exp.astype(BF)
            mixed = jnp.dot(prompt_exp.astype(BF), latent[...], preferred_element_type=F32)
            mixed_own = jnp.concatenate(
                [
                    jnp.dot(own_weight[:128], fresh[:128, :], preferred_element_type=F32),
                    jnp.dot(own_weight[128:], fresh[128:, :], preferred_element_type=F32),
                ],
                axis=0,
            )
            mixed = ((mixed + mixed_own) * factor).astype(BF)
            out = jnp.dot(mixed, vu[:, i * 128 : (i + 1) * 128], preferred_element_type=F32)
            outs.append(out.reshape(32, 8, 128))
        o_send[pair] = jnp.concatenate(outs, axis=1).astype(BF)

        @pl.loop(1, 32)
        def _(d):
            there = lax.rem(h + d, 32)
            remote(o_send.at[pair, there], out_ref.at[pair, h], o_ssem.at[pair], o_rsem.at[pair], (g, there)).start()

        keep = pltpu.make_async_copy(o_send.at[pair, h], out_ref.at[pair, h], local_sem.at[5 + pair])
        keep.start()

    for copy in w_out + wc_out + k_out + q_out + qy_out + kz_out + p_out + pz_out + pg_out + py_out:
        copy.wait_send()
    for pair in range(2):
        pltpu.make_async_copy(o_send.at[pair, h], out_ref.at[pair, h], local_sem.at[5 + pair]).wait()
        whole = remote(
            o_send.at[pair, pl.ds(0, 31)], out_ref.at[pair, pl.ds(0, 31)], o_ssem.at[pair], o_rsem.at[pair], sibling
        )
        whole.wait_send()
        whole.wait_recv()


def local(
    query_latent, response_keys, prompt_cache, owners, lengths, w_query_plain, w_query_rotary, w_key_up, w_value_up
):
    cos_table, sin_table = rotary_tables()
    vmem = pl.BlockSpec(memory_space=pltpu.VMEM)
    smem = pl.BlockSpec(memory_space=pltpu.SMEM)
    hbm = pl.BlockSpec(memory_space=pl.ANY)
    dma = pltpu.SemaphoreType.DMA
    gathered = pl.pallas_call(
        kernel,
        out_shape=jax.ShapeDtypeStruct((2, 32, 16, 128), BF),
        in_specs=[smem, vmem, vmem, vmem, vmem, vmem, hbm, hbm, hbm, hbm, hbm],
        out_specs=vmem,
        scratch_shapes=[
            pltpu.VMEM((QLAT, 512), BF),
            pltpu.VMEM((QLAT, 256), BF),
            pltpu.VMEM((512, 512), BF),
            pltpu.VMEM((512, 512), BF),
            pltpu.VMEM((1, 147456), BF),
            pltpu.VMEM((PLEN, 512), F32),
            pltpu.VMEM((16, 768), BF),
            pltpu.VMEM((16, 384), BF),
            pltpu.VMEM((32, 16, 768), BF),
            pltpu.VMEM((NY, NZ, 16, 384), BF),
            pltpu.VMEM((NY, NZ, 16, 256), BF),
            pltpu.VMEM((NY, 2, 16, 128), BF),
            pltpu.VMEM((NY, NZ, 16, 256), BF),
            pltpu.VMEM((NY, 2, 16, 128), BF),
            pltpu.VMEM((NZ, 16, 384), BF),
            pltpu.VMEM((NZ, 16, 384), BF),
            pltpu.VMEM((NY, NZ, 16, 384), BF),
            pltpu.VMEM((TOK, QLAT), BF),
            pltpu.VMEM((TOK, 512), BF),
            pltpu.VMEM((TOK, 128), BF),
            pltpu.VMEM((PLEN, 512), BF),
            pltpu.VMEM((128, PLEN), BF),
            pltpu.VMEM((TOK, 512), BF),
            pltpu.VMEM((TOK, 256), BF),
            pltpu.VMEM((4, TOK, 512), BF),
            pltpu.VMEM((2, 32, 16, 128), BF),
            dma((7,)),
            dma((4, 2)),
            dma((4, 2)),
            dma((4, 2)),
            dma((4, 2)),
            dma((8,)),
            dma((8,)),
            dma((4,)),
            dma((4,)),
            dma((4,)),
            dma((4,)),
            dma((8,)),
            dma((8,)),
            dma((4, 2)),
            dma((4, 2)),
            dma((8,)),
            dma((8,)),
            dma((8,)),
            dma((8,)),
            dma((4, 2)),
            dma((4, 2)),
            dma((2,)),
            dma((2,)),
        ],
        compiler_params=pltpu.CompilerParams(collective_id=0, has_side_effects=True, vmem_limit_bytes=40 << 20),
    )(
        owners,
        query_latent,
        response_keys,
        lengths,
        jnp.asarray(cos_table),
        jnp.asarray(sin_table),
        prompt_cache,
        w_query_plain,
        w_query_rotary,
        w_key_up,
        w_value_up,
    )
    return gathered.reshape(2, 32, 2, 8, 128).transpose(3, 1, 0, 2, 4).reshape(8, 16384)


def solution(mesh):
    return jax.shard_map(
        local,
        mesh=mesh,
        in_specs=(
            P(("group", "head"), None),
            P(("group", "head"), None),
            P(("group", "head"), None),
            P("group"),
            P("group", None),
            P("group", "head"),
            P("group", "head"),
            P("head", None),
            P(None, "head"),
        ),
        out_specs=P(("group", "head"), None),
        check_vma=False,
    )
```

time: 200 us -> 57.4 us (0.29)
  blocking collectives: 132 us -> 0 us
  Pallas kernels: 0 us -> 47.3 us
  waiting for transfers between devices: 35.8 us -> 0 us
  between operations: 15.7 us -> 0.7 us
  matrix products: 8.66 us -> 0 us
  local copies, waits for them, and re-layouts: 5.69 us -> 9.02 us
  other arithmetic: 2.31 us -> 0 us
    all_gather x3 -> x0, blocking collectives: 115 us -> none  [the longest x1 53.8 us: local(): lax.all_gather(response_keys, 'head', axis=0, tiled=True)]
    pallas_call x0 -> x1, Pallas kernels: none -> 47.3 us  [local(): pl.pallas_call(kernel, out_shape=jax.ShapeDtypeStruct((2, 32, 16, 128), B...]
    psum x1 -> x0, waiting for transfers between devices: 35.2 us -> none  [broadcast(): return lax.psum(kept, axis)]
    all_to_all x1 -> x0, blocking collectives: 16.5 us -> none  [local(): lax.all_to_all(outputs, 'head', split_axis=0, concat_axis=1, tiled=True)]
    dot_general x9 -> x0, matrix products: 8.66 us -> none  [the longest x1 2.39 us: attend(): jnp.einsum('htl,lhv->thv', mixed, value_up, preferred_element_type=jnp.fl...]
    unnamed x9 -> x20, local copies, waits for them, and re-layouts: 0.72 us -> 8.3 us
    slice x2 -> x0, local copies, waits for them, and re-layouts: 3.59 us -> none  [the longest x1 2.57 us: local(): latent = cached[:PLEN * LAT].reshape(PLEN, LAT)]
  transfers between devices with their start and end apart: 2 -> 0, of which waited for: 1 -> 0; matrix products, arithmetic and copies ran while one was open for 3% -> 0% of each run, Pallas kernels for 0% -> 0%
where the time goes in v1:
time: 57.4 us; the launch traced here: 57 us
  Pallas kernels  47.3 us (82%)
  local copies, waits for them, and re-layouts  9.02 us (16%)
  between operations  0.7 us (1%)
    pallas_call x1, Pallas kernels, local(): pl.pallas_call(kernel, out_shape=jax.ShapeDtypeStruct((2, 32, 16, 128), B...  47.3 us
    unnamed x20, local copies, waits for them, and re-layouts  8.3 us

profile of v1, /device:TPU:2, one launch (start us, length us, event | category | flops | bytes accessed | tf_op | source)
XLA Modules:
  0.0 57.0 jit_solution(5698793347847355929)
XLA Ops:
  0.0 0.0 copy-start.9
  0.7 0.0 copy-done.9
  0.7 0.0 copy-start
  0.7 1.1 %copy-done = bf16[1,147456]{1,0:T(2,128)(2,1)S(1)} copy-done((bf16[1,147456]{1,0:T(2,128)(2,1)S(1)}, bf16[1,147456]{1,0:T(2,128)(2,1)}, u32[]{:S(2)}) %copy-start) | copy-done | bytes 294936
  1.7 0.0 copy-start.1
  1.7 1.0 %copy-done.1 = bf16[512,512]{1,0:T(8,128)(2,1)S(1)} copy-done((bf16[512,512]{1,0:T(8,128)(2,1)S(1)}, bf16[512,512]{1,0:T(8,128)(2,1)}, u32[]{:S(2)}) %copy-start.1) | copy-done | bytes 524312
  2.8 0.0 copy-start.2
  2.8 1.0 %copy-done.2 = bf16[512,512]{1,0:T(8,128)(2,1)S(1)} copy-done((bf16[512,512]{1,0:T(8,128)(2,1)S(1)}, bf16[512,512]{1,0:T(8,128)(2,1)}, u32[]{:S(2)}) %copy-start.2) | copy-done | bytes 524312
  3.8 0.0 copy-start.3
  3.8 0.9 %copy-done.3 = f32[256,256]{1,0:T(8,128)S(1)} copy-done((f32[256,256]{1,0:T(8,128)S(1)}, f32[256,256]{1,0:T(8,128)}, u32[]{:S(2)}) %copy-start.3) | copy-done | bytes 262168
  4.8 0.0 copy-start.4
  4.8 0.9 %copy-done.4 = f32[256,256]{1,0:T(8,128)S(1)} copy-done((f32[256,256]{1,0:T(8,128)S(1)}, f32[256,256]{1,0:T(8,128)}, u32[]{:S(2)}) %copy-start.4) | copy-done | bytes 262168
  5.7 0.0 copy-start.5
  5.7 0.9 %copy-done.5 = bf16[192,512]{1,0:T(8,128)(2,1)S(1)} copy-done((bf16[192,512]{1,0:T(8,128)(2,1)S(1)}, bf16[192,512]{1,0:T(8,128)(2,1)}, u32[]{:S(2)}) %copy-start.5) | copy-done | bytes 196632
  6.7 0.0 copy-start.6
  6.7 0.9 %copy-done.6 = bf16[192,256]{1,0:T(8,128)(2,1)S(1)} copy-done((bf16[192,256]{1,0:T(8,128)(2,1)S(1)}, bf16[192,256]{1,0:T(8,128)(2,1)}, u32[]{:S(2)}) %copy-start.6) | copy-done | bytes 98328
  7.5 0.0 copy-start.7
  7.6 0.7 %copy-done.7 = bf16[8,1536]{1,0:T(8,128)(2,1)S(1)} copy-done((bf16[8,1536]{1,0:T(8,128)(2,1)S(1)}, bf16[8,1536]{1,0:T(8,128)(2,1)}, u32[]{:S(2)}) %copy-start.7) | copy-done | bytes 24600
  8.3 0.0 copy-start.8
  8.3 0.7 %copy-done.8 = bf16[8,576]{1,0:T(8,128)(2,1)S(1)} copy-done((bf16[8,576]{1,0:T(8,128)(2,1)S(1)}, bf16[8,576]{1,0:T(8,128)(2,1)}, u32[]{:S(2)}) %copy-start.8) | copy-done | bytes 9240
  9.0 47.3 %shard_map.109 = bf16[2,32,16,128]{3,2,1,0:T(8,128)(2,1)S(1)} custom-call(s32[1]{0:T(128)S(6)} %copy.13.owner_ref, bf16[8,1536]{1,0:T(8,128)(2,1)S(1)} %copy-done.7, bf16[8,576]{1,0:T(8,128)(2,1)S(1)} %copy-done.8, s32[1,16]{1,0:T(1,128)S(1)} %copy-done.9, f32[256,256]{1,0:T(8,128)S(1)} %copy-done.4, f32[256,256]{1,0:T(8,128)S(1)} %copy-done.3, ...), custom_call_target="tpu_custom_call" | custom-call | tf_op jit(solution)/shard_map/pallas_call | solution.py:325
  56.3 0.7 %copy.12 = bf16[8,32,2,2,128]{4,0,3,2,1:T(8,128)(2,1)} copy(bf16[8,32,2,2,128]{4,0,3,1,2:T(8,128)(2,1)S(1)} %bitcast.4) | data formatting | bytes 524288 | tf_op jit(solution)/shard_map/transpose | solution.py:395
Async XLA Ops:
  0.0 0.7 %copy-start.9 = (s32[1,16]{1,0:T(1,128)S(1)}, s32[1,16]{1,0:T(1,128)}, u32[]{:S(2)}) copy-start(s32[1,16]{1,0:T(1,128)} %length_ref.1) | copy-start | bytes 196
  0.7 1.1 %copy-start = (bf16[1,147456]{1,0:T(2,128)(2,1)S(1)}, bf16[1,147456]{1,0:T(2,128)(2,1)}, u32[]{:S(2)}) copy-start(bf16[1,147456]{1,0:T(2,128)(2,1)} %prompt_hbm.1) | copy-start | bytes 884740
  1.7 1.0 %copy-start.1 = (bf16[512,512]{1,0:T(8,128)(2,1)S(1)}, bf16[512,512]{1,0:T(8,128)(2,1)}, u32[]{:S(2)}) copy-start(bf16[512,512]{1,0:T(8,128)(2,1)} %ku_hbm.1) | copy-start | bytes 1572868
  2.8 1.0 %copy-start.2 = (bf16[512,512]{1,0:T(8,128)(2,1)S(1)}, bf16[512,512]{1,0:T(8,128)(2,1)}, u32[]{:S(2)}) copy-start(bf16[512,512]{1,0:T(8,128)(2,1)} %vu_hbm.1) | copy-start | bytes 1572868
  3.8 0.9 %copy-start.3 = (f32[256,256]{1,0:T(8,128)S(1)}, f32[256,256]{1,0:T(8,128)}, u32[]{:S(2)}) copy-start(f32[256,256]{1,0:T(8,128)} %constant.5.clone.sin_ref) | copy-start | bytes 786436
  4.8 0.9 %copy-start.4 = (f32[256,256]{1,0:T(8,128)S(1)}, f32[256,256]{1,0:T(8,128)}, u32[]{:S(2)}) copy-start(f32[256,256]{1,0:T(8,128)} %constant.4.clone.cos_ref) | copy-start | bytes 786436
  5.7 0.9 %copy-start.5 = (bf16[192,512]{1,0:T(8,128)(2,1)S(1)}, bf16[192,512]{1,0:T(8,128)(2,1)}, u32[]{:S(2)}) copy-start(bf16[192,512]{1,0:T(8,128)(2,1)} %wp_hbm.1) | copy-start | bytes 589828
  6.7 0.9 %copy-start.6 = (bf16[192,256]{1,0:T(8,128)(2,1)S(1)}, bf16[192,256]{1,0:T(8,128)(2,1)}, u32[]{:S(2)}) copy-start(bf16[192,256]{1,0:T(8,128)(2,1)} %wr_hbm.1) | copy-start | bytes 294916
  7.5 0.7 %copy-start.7 = (bf16[8,1536]{1,0:T(8,128)(2,1)S(1)}, bf16[8,1536]{1,0:T(8,128)(2,1)}, u32[]{:S(2)}) copy-start(bf16[8,1536]{1,0:T(8,128)(2,1)} %query_ref.1) | copy-start | bytes 73732
  8.3 0.7 %copy-start.8 = (bf16[8,576]{1,0:T(8,128)(2,1)S(1)}, bf16[8,576]{1,0:T(8,128)(2,1)}, u32[]{:S(2)}) copy-start(bf16[8,576]{1,0:T(8,128)(2,1)} %keys_ref.1) | copy-start | bytes 27652

commit v2 on v1

v2 whole, which is shorter than its diff:
```python
import math

import jax
import jax.numpy as jnp
import numpy as np
from jax import lax
from jax.experimental import pallas as pl
from jax.experimental.pallas import tpu as pltpu
from jax.sharding import PartitionSpec as P

MESH = pl.DeviceIdType.MESH
LAT = 512
ROPE = 64
NOPE = 128
VDIM = 128
QLAT = 1536
PLEN = 256
RTOK = 16
TOK = 256
NX, NY, NZ = 4, 4, 8
SHARD = 192
HALF = 96
BF = jnp.bfloat16
F32 = jnp.float32
SCALE = 1.0 / math.sqrt(NOPE + ROPE)
LOG2E = 1.4426950408889634


def rotary_tables():
    position = (PLEN + np.arange(RTOK)).astype(np.float32)
    inverse = np.exp(np.arange(32).astype(np.float32) * np.float32(-2.0 * math.log(10000.0) / ROPE))
    angle = (position[:, None] * inverse[None, :].astype(np.float32)).astype(np.float32)
    cosine, sine = np.cos(angle), np.sin(angle)
    cos_table = np.tile(np.concatenate([cosine, cosine], 1), (1, 4))
    sin_table = np.tile(np.concatenate([-sine, sine], 1), (1, 4))
    return np.concatenate([cos_table, sin_table], 0).astype(np.float32)


def dot_nt(a, b):
    return lax.dot_general(a, b, (((1,), (1,)), ((), ())), preferred_element_type=F32)


def kernel(
    owner_hbm, query_hbm, keys_hbm, length_hbm, table_hbm, prompt_hbm, wp_hbm, wr_hbm, ku_hbm, vu_hbm,
    out_ref,
    owner_ref, query_ref, keys_ref, length_ref, table_ref, w, ku, vu, flat, stage, q_send, k_send, r_own, qb, kl, kt, kr,
    p_send, r_send, p_recv, r_recv, z_send, z_recv, pl_buf,
    x_buf, fresh, fresh_rot, latent, rotary, plain, turned, absorbed, own_buf, o_send,
    local_sem, wx_send, wx_recv, wf_send, wf_recv, wc_send, wc_recv,
    qz_send, qz_recv, qy_send, qy_recv, ky_send, ky_recv, kz_send, kz_recv,
    pa_send, pa_recv, pz_send, pz_recv, pg_send, pg_recv, py_send, py_recv,
    o_ssem, o_rsem,
):
    g = lax.axis_index("group")
    h = lax.axis_index("head")
    x, c = g // 2, g % 2
    y, z = h // NZ, h % NZ

    def at_x(d):
        return (lax.rem(x + d, NX) * 2 + c, h)

    def at_y(d):
        return (g, lax.rem(y + d, NY) * NZ + z)

    def at_z(d):
        return (g, y * NZ + lax.rem(z + d, NZ))

    sibling = (x * 2 + 1 - c, h)
    y_order = (1, 3, 2)
    z_order = (4, 3, 5, 2, 6, 1, 7)

    def remote(src, dst, ssem, rsem, device):
        return pltpu.make_async_remote_copy(src, dst, ssem, rsem, device_id=device, device_id_type=MESH)

    barrier = pltpu.get_barrier_semaphore()
    peers = [sibling] + [at_x(d) for d in (1, 3)] + [at_y(d) for d in y_order] + [at_z(d) for d in z_order]
    for peer in peers:
        pl.semaphore_signal(barrier, inc=1, device_id=peer, device_id_type=MESH)

    def half_rows(dx, core, half):
        start = (lax.rem(x + dx + NX, NX) * 2 + core) * SHARD + half * HALF
        return pl.ds(pl.multiple_of(start, 32), HALF)

    mine = pl.ds(pl.multiple_of(g * SHARD, 64), SHARD)
    flat_copy = pltpu.make_async_copy(prompt_hbm, flat, local_sem.at[0])
    query_copy = pltpu.make_async_copy(query_hbm, query_ref, local_sem.at[7])
    keys_copy = pltpu.make_async_copy(keys_hbm, keys_ref, local_sem.at[8])
    wp_copy = pltpu.make_async_copy(wp_hbm, w.at[mine, 0:512], local_sem.at[3])
    wr_copy = pltpu.make_async_copy(wr_hbm, w.at[mine, 512:768], local_sem.at[4])
    owner_copy = pltpu.make_async_copy(owner_hbm, owner_ref, local_sem.at[9])
    length_copy = pltpu.make_async_copy(length_hbm, length_ref, local_sem.at[10])
    table_copy = pltpu.make_async_copy(table_hbm, table_ref, local_sem.at[11])
    ku_copy = pltpu.make_async_copy(ku_hbm, ku, local_sem.at[1])
    vu_copy = pltpu.make_async_copy(vu_hbm, vu, local_sem.at[2])
    for copy in (
        flat_copy, query_copy, keys_copy, wp_copy, wr_copy, owner_copy, length_copy, table_copy, ku_copy, vu_copy
    ):
        copy.start()

    flat_copy.wait()

    @pl.loop(0, PLEN // 8)
    def _(block):
        for r in range(8):
            row = flat[0:1, pl.ds(pl.multiple_of(block * 4096 + r * 512, 512), 512)].astype(F32)
            stage[pl.ds(block * 8 + r, 1), :] = row
        both = stage[pl.ds(pl.multiple_of(block * 8, 8), 8), :]
        p_send[pl.ds(block // 8, 1), pl.ds(block % 8, 1)] = jnp.concatenate(
            [both[:, :256], both[:, 256:]], axis=0
        ).astype(BF)[None, None]

    @pl.loop(0, NY)
    def _(j):
        for r in range(16):
            row = flat[0:1, pl.ds(pl.multiple_of(PLEN * LAT + j * 4096 + r * 256, 256), 256)].astype(F32)
            stage[pl.ds(r, 1), 0:256] = row
        both = stage[0:16, 0:256].astype(BF)
        r_send[pl.ds(j, 1), 0:1] = both[None, None, :, :128]
        r_send[pl.ds(j, 1), 1:2] = both[None, None, :, 128:]

    p_recv[pl.ds(y, 1)] = p_send[pl.ds(y, 1)]
    r_recv[pl.ds(y, 1)] = r_send[pl.ds(y, 1)]

    query_copy.wait()
    query = query_ref[...].astype(F32)
    packed = jnp.concatenate([query[:, :768], query[:, 768:]], axis=0).astype(BF)
    q_send[...] = packed
    qb[pl.ds(h, 1)] = packed[None]
    keys_copy.wait()
    keys = keys_ref[...].astype(F32)
    packed = jnp.concatenate([keys[:, :256], keys[:, 256:512]], axis=0).astype(BF)
    k_send[...] = packed
    kl[pl.ds(y, 1), pl.ds(z, 1)] = packed[None, None]
    rot = jnp.concatenate([keys[:, 512:], keys[:, 512:]], axis=1)
    packed = jnp.concatenate([rot, rot], axis=0).astype(BF)
    r_own[...] = packed
    kt[pl.ds(y, 1)] = packed[None]
    wp_copy.wait()
    wr_copy.wait()

    pl.semaphore_wait(barrier, len(peers))

    p_out, k_out = [], []
    for d in y_order:
        there = lax.rem(y + d, NY)
        k_out.append(remote(k_send, kl.at[y, z], ky_send.at[d, 0], ky_recv.at[d, 0], at_y(d)))
        k_out.append(remote(r_own, kt.at[y], ky_send.at[d, 1], ky_recv.at[d, 1], at_y(d)))
        p_out.append(remote(p_send.at[there], p_recv.at[y], pa_send.at[d, 0], pa_recv.at[d, 0], at_y(d)))
        p_out.append(remote(r_send.at[there], r_recv.at[y], pa_send.at[d, 1], pa_recv.at[d, 1], at_y(d)))
    q_out = [remote(q_send, qb.at[h], qz_send.at[d], qz_recv.at[d], at_z(d)) for d in z_order]
    w_out = []
    for step in range(2):
        for d in (1, 3):
            half = step if d == 1 else 1 - step
            rows = w.at[half_rows(0, c, half)]
            w_out.append(remote(rows, rows, wx_send.at[d, half], wx_recv.at[d, half], at_x(d)))
    for copy in p_out + k_out + q_out + w_out:
        copy.start()
    wc_out = []

    def to_sibling(dx, half):
        rows = w.at[half_rows(dx, c, half)]
        wc_out.append(remote(rows, rows, wc_send.at[dx, half], wc_recv.at[dx, half], sibling))
        wc_out[-1].start()

    def from_sibling(dx, half):
        rows = w.at[half_rows(dx, 1 - c, half)]
        remote(rows, rows, wc_send.at[dx, half], wc_recv.at[dx, half], sibling).wait_recv()

    def arrived(d, half):
        rows = w.at[half_rows(NX - d, c, half)]
        remote(rows, rows, wx_send.at[d, half], wx_recv.at[d, half], at_x(d)).wait_recv()

    to_sibling(0, 0)
    to_sibling(0, 1)

    for copy in k_out:
        copy.wait_recv()
    tiles = kt[...].astype(F32)
    tile_row = lax.broadcasted_iota(jnp.int32, (16, 128), 0)
    tile_lane = lax.broadcasted_iota(jnp.int32, (16, 128), 1)
    upper = jnp.where(tile_lane < 64, tiles[0], tiles[1])
    lower = jnp.where(tile_lane < 64, tiles[2], tiles[3])
    kr[pl.ds(z, 1)] = jnp.where(tile_row < 8, upper, lower).astype(BF)[None]
    kz_out = []
    for d in z_order:
        kz_out.append(remote(kl.at[:, z], kl.at[:, z], kz_send.at[d, 0], kz_recv.at[d, 0], at_z(d)))
        kz_out.append(remote(kr.at[z], kr.at[z], kz_send.at[d, 1], kz_recv.at[d, 1], at_z(d)))

    wf_out = []

    def pass_on(d, half):
        arrived(d, half)
        rows = w.at[half_rows(NX - d, c, half)]
        wf_out.append(remote(rows, rows, wf_send.at[half], wf_recv.at[half], at_x(d)))
        wf_out[-1].start()
        to_sibling(NX - d, half)

    pass_on(1, 0)
    pass_on(3, 1)

    owner_copy.wait()
    owner = owner_ref[0]
    for copy in p_out:
        copy.wait_recv()
    chosen = p_recv[owner // NZ]
    chosen_rot = r_recv[owner // NZ]
    for k in range(NZ):
        z_send[k] = jnp.concatenate([chosen[k], chosen_rot[k % 2]], axis=1)
    pz_out = []
    for d in z_order:
        pz_out.append(remote(z_send.at[lax.rem(z + d, NZ)], z_recv.at[z], pz_send.at[d], pz_recv.at[d], at_z(d)))
    for copy in pz_out:
        copy.start()
    z_recv[pl.ds(z, 1)] = z_send[pl.ds(z, 1)]

    for copy in q_out:
        copy.wait_recv()
    row = pl.ds(pl.multiple_of(y * NZ, NZ), NZ)
    qy_out = [remote(qb.at[row], qb.at[row], qy_send.at[d], qy_recv.at[d], at_y(d)) for d in y_order]
    for copy in qy_out + kz_out:
        copy.start()

    for copy in pz_out:
        copy.wait_recv()
    pl_buf[pl.ds(y, 1), pl.ds(z, 1)] = z_recv[owner % NZ][None, None]
    pg_out = [remote(pl_buf.at[y, z], pl_buf.at[y, z], pg_send.at[d], pg_recv.at[d], at_z(d)) for d in z_order]
    for copy in pg_out:
        copy.start()

    arrived(1, 1)
    to_sibling(3, 1)
    arrived(3, 0)
    to_sibling(1, 0)
    for half in range(2):
        rows = w.at[half_rows(2, c, half)]
        remote(rows, rows, wf_send.at[half], wf_recv.at[half], sibling).wait_recv()
        to_sibling(2, half)

    for copy in pg_out:
        copy.wait_recv()
    py_out = []
    for d in y_order:
        part = pl_buf.at[y, :, :, 0:256]
        py_out.append(remote(part, part, py_send.at[d, 0], py_recv.at[d, 0], at_y(d)))
        part = pl_buf.at[y, 0:2, :, 256:384]
        py_out.append(remote(part, part, py_send.at[d, 1], py_recv.at[d, 1], at_y(d)))
    for copy in py_out:
        copy.start()

    for copy in qy_out:
        copy.wait_recv()
    gathered = qb[...].astype(F32)
    x_buf[:, :768] = gathered[:, :8].reshape(TOK, 768).astype(BF)
    x_buf[:, 768:] = gathered[:, 8:].reshape(TOK, 768).astype(BF)
    for dx in range(NX):
        for half in range(2):
            from_sibling(dx, half)
    both = jnp.dot(x_buf[...], w[...], preferred_element_type=F32)
    plain[...] = both[:, :512].astype(BF)
    spun = both[:, 512:]
    lane = lax.broadcasted_iota(jnp.int32, (TOK, 256), 1)
    swapped = jnp.where(lane % 64 < 32, pltpu.roll(spun, 224, 1), pltpu.roll(spun, 32, 1))
    table_copy.wait()
    cosine = jnp.broadcast_to(table_ref[:16][None], (16, 16, 256)).reshape(TOK, 256)
    sine = jnp.broadcast_to(table_ref[16:][None], (16, 16, 256)).reshape(TOK, 256)
    turned[...] = (spun * cosine + swapped * sine).astype(BF)

    ku_copy.wait()
    for i in range(4):
        absorbed[i] = jnp.dot(
            plain[:, i * 128 : (i + 1) * 128], ku[i * 128 : (i + 1) * 128, :], preferred_element_type=F32
        ).astype(BF)

    for copy in kz_out:
        copy.wait_recv()
    gathered = kl[...].astype(F32).reshape(32, 16, 256)
    fresh[:, :256] = gathered[:, :8].reshape(TOK, 256).astype(BF)
    fresh[:, 256:] = gathered[:, 8:].reshape(TOK, 256).astype(BF)
    gathered = kr[...].astype(F32)
    rot_lane = lax.broadcasted_iota(jnp.int32, (64, 128), 1)
    for j in range(NY):
        piece = gathered[:, (j // 2) * 8 : (j // 2) * 8 + 8].reshape(64, 128)
        piece = jnp.where((rot_lane < 64) if j % 2 == 0 else (rot_lane >= 64), piece, 0.0)
        fresh_rot[j * 64 : (j + 1) * 64, :] = (piece + pltpu.roll(piece, 64, 1)).astype(BF)

    length_copy.wait()
    lengths = jnp.broadcast_to(length_ref[...], (TOK, 16))
    token = lax.broadcasted_iota(jnp.int32, (TOK, 16), 0)
    slot = lax.broadcasted_iota(jnp.int32, (TOK, 16), 1)
    limit = jnp.sum(jnp.where(token // RTOK == slot, lengths, 0).astype(F32), axis=1, keepdims=True)
    place = (lax.broadcasted_iota(jnp.int32, (TOK, 1), 0) % RTOK).astype(F32)
    live = place < limit

    t_half = lax.broadcasted_iota(jnp.int32, (128, 128), 0)
    s_half = lax.broadcasted_iota(jnp.int32, (128, 128), 1)
    allowed = (t_half // RTOK == s_half // RTOK) & (s_half <= t_half)
    pair_lane = lax.broadcasted_iota(jnp.int32, (TOK, 128), 1)

    def own_turned(i):
        mine_lanes = (pair_lane < 64) if i % 2 == 0 else (pair_lane >= 64)
        part = turned[:, (i // 2) * 128 : (i // 2 + 1) * 128].astype(F32)
        return jnp.where(mine_lanes, part, 0.0).astype(BF)

    for i in range(4):
        t = own_turned(i)
        for half in range(2):
            part = slice(half * 128, (half + 1) * 128)
            scores = dot_nt(absorbed[i, part, :], fresh[part, :]) + dot_nt(t[part], fresh_rot[part, :])
            own_buf[i, part, :] = jnp.where(allowed, scores, -jnp.inf)
    vu_copy.wait()

    for copy in py_out:
        copy.wait_recv()
    gathered = pl_buf[:, :, :, :256].astype(F32).reshape(32, 16, 256)
    latent[:, :256] = gathered[:, :8].reshape(PLEN, 256).astype(BF)
    latent[:, 256:] = gathered[:, 8:].reshape(PLEN, 256).astype(BF)
    for j in range(NY):
        both = jnp.concatenate([pl_buf[j, 0, :, 256:], pl_buf[j, 1, :, 256:]], axis=1)
        rotary[j * 16 : (j + 1) * 16, :] = both
        rotary[64 + j * 16 : 64 + (j + 1) * 16, :] = both

    for pair in range(2):
        outs = []
        for sub in range(2):
            i = pair * 2 + sub
            prompt_scores = dot_nt(absorbed[i], latent[...]) + jnp.dot(
                own_turned(i), rotary[...], preferred_element_type=F32
            )
            own_scores = own_buf[i]
            top = jnp.max(
                jnp.maximum(jnp.maximum(prompt_scores[:, :128], prompt_scores[:, 128:]), own_scores),
                axis=1,
                keepdims=True,
            )
            prompt_exp = jnp.exp2((prompt_scores - top) * (SCALE * LOG2E))
            own_exp = jnp.exp2((own_scores - top) * (SCALE * LOG2E))
            total = jnp.sum(prompt_exp[:, :128] + prompt_exp[:, 128:] + own_exp, axis=1, keepdims=True)
            factor = jnp.where(live, 1.0 / total, 0.0)
            own_weight = own_exp.astype(BF)
            mixed = jnp.dot(prompt_exp.astype(BF), latent[...], preferred_element_type=F32)
            mixed_own = jnp.concatenate(
                [
                    jnp.dot(own_weight[:128], fresh[:128, :], preferred_element_type=F32),
                    jnp.dot(own_weight[128:], fresh[128:, :], preferred_element_type=F32),
                ],
                axis=0,
            )
            mixed = ((mixed + mixed_own) * factor).astype(BF)
            out = jnp.dot(mixed, vu[:, i * 128 : (i + 1) * 128], preferred_element_type=F32)
            outs.append(out.reshape(32, 8, 128))
        o_send[pair] = jnp.concatenate(outs, axis=1).astype(BF)

        @pl.loop(1, 32)
        def _(d):
            there = lax.rem(h + d, 32)
            remote(o_send.at[pair, there], out_ref.at[pair, h], o_ssem.at[pair], o_rsem.at[pair], (g, there)).start()

        keep = pltpu.make_async_copy(o_send.at[pair, h], out_ref.at[pair, h], local_sem.at[5 + pair])
        keep.start()

    for copy in w_out + wf_out + wc_out + k_out + q_out + qy_out + kz_out + p_out + pz_out + pg_out + py_out:
        copy.wait_send()
    for pair in range(2):
        pltpu.make_async_copy(o_send.at[pair, h], out_ref.at[pair, h], local_sem.at[5 + pair]).wait()
        whole = remote(
            o_send.at[pair, pl.ds(0, 31)], out_ref.at[pair, pl.ds(0, 31)], o_ssem.at[pair], o_rsem.at[pair], sibling
        )
        whole.wait_send()
        whole.wait_recv()


def local(
    query_latent, response_keys, prompt_cache, owners, lengths, w_query_plain, w_query_rotary, w_key_up, w_value_up
):
    vmem = pl.BlockSpec(memory_space=pltpu.VMEM)
    hbm = pl.BlockSpec(memory_space=pl.ANY)
    dma = pltpu.SemaphoreType.DMA
    gathered = pl.pallas_call(
        kernel,
        out_shape=jax.ShapeDtypeStruct((2, 32, 16, 128), BF),
        in_specs=[hbm] * 10,
        out_specs=vmem,
        scratch_shapes=[
            pltpu.SMEM((1,), jnp.int32),
            pltpu.VMEM((8, QLAT), BF),
            pltpu.VMEM((8, 576), BF),
            pltpu.VMEM((1, 16), jnp.int32),
            pltpu.VMEM((32, 256), F32),
            pltpu.VMEM((QLAT, 768), BF),
            pltpu.VMEM((512, 512), BF),
            pltpu.VMEM((512, 512), BF),
            pltpu.VMEM((1, 147456), BF),
            pltpu.VMEM((PLEN, 512), F32),
            pltpu.VMEM((16, 768), BF),
            pltpu.VMEM((16, 256), BF),
            pltpu.VMEM((16, 128), BF),
            pltpu.VMEM((32, 16, 768), BF),
            pltpu.VMEM((NY, NZ, 16, 256), BF),
            pltpu.VMEM((NY, 16, 128), BF),
            pltpu.VMEM((NZ, 16, 128), BF),
            pltpu.VMEM((NY, NZ, 16, 256), BF),
            pltpu.VMEM((NY, 2, 16, 128), BF),
            pltpu.VMEM((NY, NZ, 16, 256), BF),
            pltpu.VMEM((NY, 2, 16, 128), BF),
            pltpu.VMEM((NZ, 16, 384), BF),
            pltpu.VMEM((NZ, 16, 384), BF),
            pltpu.VMEM((NY, NZ, 16, 384), BF),
            pltpu.VMEM((TOK, QLAT), BF),
            pltpu.VMEM((TOK, 512), BF),
            pltpu.VMEM((TOK, 128), BF),
            pltpu.VMEM((PLEN, 512), BF),
            pltpu.VMEM((128, PLEN), BF),
            pltpu.VMEM((TOK, 512), BF),
            pltpu.VMEM((TOK, 256), BF),
            pltpu.VMEM((4, TOK, 512), BF),
            pltpu.VMEM((4, TOK, 128), F32),
            pltpu.VMEM((2, 32, 16, 128), BF),
            dma((12,)),
            *[dma((4, 2))] * 2,
            *[dma((2,))] * 2,
            *[dma((4, 2))] * 2,
            *[dma((8,))] * 2,
            *[dma((4,))] * 2,
            *[dma((4, 2))] * 2,
            *[dma((8, 2))] * 2,
            *[dma((4, 2))] * 2,
            *[dma((8,))] * 4,
            *[dma((4, 2))] * 2,
            *[dma((2,))] * 2,
        ],
        compiler_params=pltpu.CompilerParams(collective_id=0, has_side_effects=True, vmem_limit_bytes=60 << 20),
    )(
        owners,
        query_latent,
        response_keys,
        lengths,
        jnp.asarray(rotary_tables()),
        prompt_cache,
        w_query_plain,
        w_query_rotary,
        w_key_up,
        w_value_up,
    )
    return gathered.reshape(2, 32, 2, 8, 128).transpose(3, 1, 0, 2, 4).reshape(8, 16384)


def solution(mesh):
    return jax.shard_map(
        local,
        mesh=mesh,
        in_specs=(
            P(("group", "head"), None),
            P(("group", "head"), None),
            P(("group", "head"), None),
            P("group"),
            P("group", None),
            P("group", "head"),
            P("group", "head"),
            P("head", None),
            P(None, "head"),
        ),
        out_specs=P(("group", "head"), None),
        check_vma=False,
    )
```

time: 57.4 us -> 46.4 us (0.81)
  local copies, waits for them, and re-layouts: 9.02 us -> 1.67 us
  Pallas kernels: 47.3 us -> 43.9 us
    unnamed x20 -> x0, local copies, waits for them, and re-layouts: 8.3 us -> none
    pallas_call x1, Pallas kernels: 47.3 us -> 43.9 us  [local(): pl.pallas_call(kernel, out_shape=jax.ShapeDtypeStruct((2, 32, 16, 128), B...]
    transpose x1, local copies, waits for them, and re-layouts: 0.72 us -> 1.67 us  [local(): gathered.reshape(2, 32, 2, 8, 128).transpose(3, 1, 0, 2, 4)]
where the time goes in v2:
time: 46.4 us; the launch traced here: 46.3 us
  Pallas kernels  43.9 us (95%)
  local copies, waits for them, and re-layouts  1.67 us (4%)
  between operations  0.66 us (1%)
    pallas_call x1, Pallas kernels, local(): pl.pallas_call(kernel, out_shape=jax.ShapeDtypeStruct((2, 32, 16, 128), B...  43.9 us
    transpose x1, local copies, waits for them, and re-layouts, local(): gathered.reshape(2, 32, 2, 8, 128).transpose(3, 1, 0, 2, 4)  1.67 us

profile of v2, /device:TPU:2, one launch (start us, length us, event | category | flops | bytes accessed | tf_op | source)
XLA Modules:
  0.0 46.3 jit_solution(1765912634550015962)
XLA Ops:
  0.7 43.9 %shard_map.100 = bf16[2,32,16,128]{3,2,1,0:T(8,128)(2,1)} custom-call(s32[1]{0:T(128)S(6)} %copy.12.owner_hbm, bf16[8,1536]{1,0:T(8,128)(2,1)} %query_hbm.1, bf16[8,576]{1,0:T(8,128)(2,1)} %keys_hbm.1, s32[1,16]{1,0:T(1,128)} %length_hbm.1, f32[32,256]{1,0:T(8,128)} %constant.2.clone.table_hbm, bf16[1,147456]{1,0:T(2,128)(2,1)} %prompt_hbm.1, ...), custom_call_target="tpu_custom_call" | custom-call | tf_op jit(solution)/shard_map/pallas_call | solution.py:379
  44.6 1.7 %copy.11 = bf16[8,32,2,2,128]{4,0,3,2,1:T(8,128)(2,1)} copy(bf16[8,32,2,2,128]{4,0,3,1,2:T(8,128)(2,1)} %bitcast.4) | data formatting | bytes 524288 | tf_op jit(solution)/shard_map/transpose | solution.py:445

commit v3 on v2

--- a/solution.py
+++ b/solution.py
@@ -47,7 +47,7 @@
     p_send, r_send, p_recv, r_recv, z_send, z_recv, pl_buf,
     x_buf, fresh, fresh_rot, latent, rotary, plain, turned, absorbed, own_buf, o_send,
     local_sem, wx_send, wx_recv, wf_send, wf_recv, wc_send, wc_recv,
-    qz_send, qz_recv, qy_send, qy_recv, ky_send, ky_recv, kz_send, kz_recv,
+    qz_send, qz_recv, qy_send, qy_recv, qf_send, qf_recv, ky_send, ky_recv, kz_send, kz_recv,
     pa_send, pa_recv, pz_send, pz_recv, pg_send, pg_recv, py_send, py_recv,
     o_ssem, o_rsem,
 ):
@@ -182,10 +182,25 @@
     upper = jnp.where(tile_lane < 64, tiles[0], tiles[1])
     lower = jnp.where(tile_lane < 64, tiles[2], tiles[3])
     kr[pl.ds(z, 1)] = jnp.where(tile_row < 8, upper, lower).astype(BF)[None]
-    kz_out = []
-    for d in z_order:
-        kz_out.append(remote(kl.at[:, z], kl.at[:, z], kz_send.at[d, 0], kz_recv.at[d, 0], at_z(d)))
-        kz_out.append(remote(kr.at[z], kr.at[z], kz_send.at[d, 1], kz_recv.at[d, 1], at_z(d)))
+    kz_out, kf_out = [], []
+
+    def at(d):
+        return lax.rem(z + d + NZ, NZ)
+
+    def key_hop(copies, n, d, source, rows):
+        part = kl.at[rows, at(source)]
+        copies.append(remote(part, part, kz_send.at[n, 0], kz_recv.at[n, 0], at_z(d)))
+        if n != 7:
+            part = kr.at[at(source)]
+            copies.append(remote(part, part, kz_send.at[n, 1], kz_recv.at[n, 1], at_z(d)))
+
+    every = slice(0, NY)
+    for n, d in enumerate((2, 6, 1, 7)):
+        key_hop(kz_out, n, d, 0, every)
+    key_hop(kf_out, 4, 6, 2, slice(0, 2))
+    key_hop(kf_out, 7, 2, -2, slice(2, 4))
+    key_hop(kf_out, 5, 1, -2, every)
+    key_hop(kf_out, 6, 7, 2, every)
 
     wf_out = []
 
@@ -196,11 +211,8 @@
         wf_out[-1].start()
         to_sibling(NX - d, half)
 
-    pass_on(1, 0)
-    pass_on(3, 1)
-
     owner_copy.wait()
-    owner = owner_ref[0]
+    owner = owner_ref[0, 0]
     for copy in p_out:
         copy.wait_recv()
     chosen = p_recv[owner // NZ]
@@ -214,10 +226,21 @@
         copy.start()
     z_recv[pl.ds(z, 1)] = z_send[pl.ds(z, 1)]
 
+    pass_on(1, 0)
+    pass_on(3, 1)
+
     for copy in q_out:
         copy.wait_recv()
-    row = pl.ds(pl.multiple_of(y * NZ, NZ), NZ)
-    qy_out = [remote(qb.at[row], qb.at[row], qy_send.at[d], qy_recv.at[d], at_y(d)) for d in y_order]
+
+    def query_rows(dy, half):
+        return qb.at[pl.ds(lax.rem(y + dy + NY, NY) * NZ + half * 4, 4)]
+
+    qy_out, qf_out = [], []
+    for step in range(2):
+        for d in (1, 3):
+            half = step if d == 1 else 1 - step
+            part = query_rows(0, half)
+            qy_out.append(remote(part, part, qy_send.at[d, half], qy_recv.at[d, half], at_y(d)))
     for copy in qy_out + kz_out:
         copy.start()
 
@@ -227,6 +250,15 @@
     pg_out = [remote(pl_buf.at[y, z], pl_buf.at[y, z], pg_send.at[d], pg_recv.at[d], at_z(d)) for d in z_order]
     for copy in pg_out:
         copy.start()
+    for copy in kz_out:
+        copy.wait_recv()
+    for copy in kf_out:
+        copy.start()
+    for n, (d, half) in enumerate(((1, 0), (3, 1))):
+        qy_out[n].wait_recv()
+        part = query_rows(-1 if d == 1 else 1, half)
+        qf_out.append(remote(part, part, qf_send.at[half], qf_recv.at[half], at_y(d)))
+        qf_out[-1].start()
 
     arrived(1, 1)
     to_sibling(3, 1)
@@ -248,7 +280,7 @@
     for copy in py_out:
         copy.start()
 
-    for copy in qy_out:
+    for copy in qy_out[2:] + qf_out:
         copy.wait_recv()
     gathered = qb[...].astype(F32)
     x_buf[:, :768] = gathered[:, :8].reshape(TOK, 768).astype(BF)
@@ -272,7 +304,7 @@
             plain[:, i * 128 : (i + 1) * 128], ku[i * 128 : (i + 1) * 128, :], preferred_element_type=F32
         ).astype(BF)
 
-    for copy in kz_out:
+    for copy in kf_out:
         copy.wait_recv()
     gathered = kl[...].astype(F32).reshape(32, 16, 256)
     fresh[:, :256] = gathered[:, :8].reshape(TOK, 256).astype(BF)
@@ -354,17 +386,17 @@
         @pl.loop(1, 32)
         def _(d):
             there = lax.rem(h + d, 32)
-            remote(o_send.at[pair, there], out_ref.at[pair, h], o_ssem.at[pair], o_rsem.at[pair], (g, there)).start()
-
-        keep = pltpu.make_async_copy(o_send.at[pair, h], out_ref.at[pair, h], local_sem.at[5 + pair])
+            remote(o_send.at[pair, there], out_ref.at[h, pair], o_ssem.at[pair], o_rsem.at[pair], (g, there)).start()
+
+        keep = pltpu.make_async_copy(o_send.at[pair, h], out_ref.at[h, pair], local_sem.at[5 + pair])
         keep.start()
 
-    for copy in w_out + wf_out + wc_out + k_out + q_out + qy_out + kz_out + p_out + pz_out + pg_out + py_out:
+    for copy in w_out + wf_out + wc_out + k_out + q_out + qy_out + qf_out + kz_out + kf_out + p_out + pz_out + pg_out + py_out:
         copy.wait_send()
     for pair in range(2):
-        pltpu.make_async_copy(o_send.at[pair, h], out_ref.at[pair, h], local_sem.at[5 + pair]).wait()
+        pltpu.make_async_copy(o_send.at[pair, h], out_ref.at[h, pair], local_sem.at[5 + pair]).wait()
         whole = remote(
-            o_send.at[pair, pl.ds(0, 31)], out_ref.at[pair, pl.ds(0, 31)], o_ssem.at[pair], o_rsem.at[pair], sibling
+            o_send.at[pair, pl.ds(0, 31)], out_ref.at[pl.ds(0, 31), pair], o_ssem.at[pair], o_rsem.at[pair], sibling
         )
         whole.wait_send()
         whole.wait_recv()
@@ -374,15 +406,15 @@
     query_latent, response_keys, prompt_cache, owners, lengths, w_query_plain, w_query_rotary, w_key_up, w_value_up
 ):
     vmem = pl.BlockSpec(memory_space=pltpu.VMEM)
-    hbm = pl.BlockSpec(memory_space=pl.ANY)
+    hbm = pl.BlockSpec(memory_space=pltpu.HBM)
     dma = pltpu.SemaphoreType.DMA
     gathered = pl.pallas_call(
         kernel,
-        out_shape=jax.ShapeDtypeStruct((2, 32, 16, 128), BF),
+        out_shape=jax.ShapeDtypeStruct((32, 2, 16, 128), BF),
         in_specs=[hbm] * 10,
-        out_specs=vmem,
+        out_specs=hbm,
         scratch_shapes=[
-            pltpu.SMEM((1,), jnp.int32),
+            pltpu.SMEM((1, 1), jnp.int32),
             pltpu.VMEM((8, QLAT), BF),
             pltpu.VMEM((8, 576), BF),
             pltpu.VMEM((1, 16), jnp.int32),
@@ -421,7 +453,8 @@
             *[dma((2,))] * 2,
             *[dma((4, 2))] * 2,
             *[dma((8,))] * 2,
-            *[dma((4,))] * 2,
+            *[dma((4, 2))] * 2,
+            *[dma((2,))] * 2,
             *[dma((4, 2))] * 2,
             *[dma((8, 2))] * 2,
             *[dma((4, 2))] * 2,
@@ -431,7 +464,7 @@
         ],
         compiler_params=pltpu.CompilerParams(collective_id=0, has_side_effects=True, vmem_limit_bytes=60 << 20),
     )(
-        owners,
+        owners.reshape(1, 1),
         query_latent,
         response_keys,
         lengths,
@@ -442,7 +475,7 @@
         w_key_up,
         w_value_up,
     )
-    return gathered.reshape(2, 32, 2, 8, 128).transpose(3, 1, 0, 2, 4).reshape(8, 16384)
+    return gathered.reshape(32, 2, 2, 8, 128).transpose(3, 0, 1, 2, 4).reshape(8, 16384)
 
 
 def solution(mesh):

time: 46.4 us -> 43.4 us (0.935)
  Pallas kernels: 43.9 us -> 40.9 us
    pallas_call x1, Pallas kernels: 43.9 us -> 40.9 us  [local(): pl.pallas_call(kernel, out_shape=jax.ShapeDtypeStruct((32, 2, 16, 128), B...]
    transpose x1 -> x0, local copies, waits for them, and re-layouts: 1.67 us -> none  [local(): gathered.reshape(2, 32, 2, 8, 128).transpose(3, 1, 0, 2, 4)]
    unnamed x0 -> x1, local copies, waits for them, and re-layouts: none -> 1.67 us
where the time goes in v3:
time: 43.4 us; the launch traced here: 43.3 us
  Pallas kernels  40.9 us (94%)
  local copies, waits for them, and re-layouts  1.67 us (4%)
  between operations  0.66 us (2%)
    pallas_call x1, Pallas kernels, local(): pl.pallas_call(kernel, out_shape=jax.ShapeDtypeStruct((32, 2, 16, 128), B...  40.9 us
    unnamed x1, local copies, waits for them, and re-layouts  1.67 us

profile of v3, /device:TPU:2, one launch (start us, length us, event | category | flops | bytes accessed | tf_op | source)
XLA Modules:
  0.0 43.3 jit_solution(17775529418650809825)
XLA Ops:
  0.7 40.9 %shard_map.100 = bf16[32,2,16,128]{3,2,1,0:T(8,128)(2,1)} custom-call(s32[1,1]{1,0:T(1,128)} %bitcast.6.owner_hbm, bf16[8,1536]{1,0:T(8,128)(2,1)} %query_hbm.1, bf16[8,576]{1,0:T(8,128)(2,1)} %keys_hbm.1, s32[1,16]{1,0:T(1,128)} %length_hbm.1, f32[32,256]{1,0:T(8,128)} %constant.2.clone.table_hbm, bf16[1,147456]{1,0:T(2,128)(2,1)} %prompt_hbm.1, ...), custom_call_target="tpu_custom_call" | custom-call | tf_op jit(solution)/shard_map/pallas_call | solution.py:411
  41.6 1.7 %copy.13 = bf16[8,16384]{1,0:T(8,128)(2,1)} copy(bf16[8,16384]{1,0:T(8,128)(2,1)} %bitcast.7) | data formatting | bytes 524288

commit v4 on v3

--- a/solution.py
+++ b/solution.py
@@ -49,7 +49,7 @@
     local_sem, wx_send, wx_recv, wf_send, wf_recv, wc_send, wc_recv,
     qz_send, qz_recv, qy_send, qy_recv, qf_send, qf_recv, ky_send, ky_recv, kz_send, kz_recv,
     pa_send, pa_recv, pz_send, pz_recv, pg_send, pg_recv, py_send, py_recv,
-    o_ssem, o_rsem,
+    o_ssem, o_rsem, ready,
 ):
     g = lax.axis_index("group")
     h = lax.axis_index("head")
@@ -67,13 +67,14 @@
 
     sibling = (x * 2 + 1 - c, h)
     y_order = (1, 3, 2)
-    z_order = (4, 3, 5, 2, 6, 1, 7)
+    z_far, z_near = (4, 3, 5), (2, 6, 1, 7)
+    z_order = z_far + z_near
 
     def remote(src, dst, ssem, rsem, device):
         return pltpu.make_async_remote_copy(src, dst, ssem, rsem, device_id=device, device_id_type=MESH)
 
     barrier = pltpu.get_barrier_semaphore()
-    peers = [sibling] + [at_x(d) for d in (1, 3)] + [at_y(d) for d in y_order] + [at_z(d) for d in z_order]
+    peers = [sibling] + [at_x(d) for d in (1, 3)] + [at_y(d) for d in y_order] + [at_z(d) for d in z_near]
     for peer in peers:
         pl.semaphore_signal(barrier, inc=1, device_id=peer, device_id_type=MESH)
 
@@ -139,6 +140,8 @@
     wr_copy.wait()
 
     pl.semaphore_wait(barrier, len(peers))
+    for d in (2, 6):
+        pl.semaphore_signal(ready, inc=1, device_id=at_z(d), device_id_type=MESH)
 
     p_out, k_out = [], []
     for d in y_order:
@@ -147,14 +150,14 @@
         k_out.append(remote(r_own, kt.at[y], ky_send.at[d, 1], ky_recv.at[d, 1], at_y(d)))
         p_out.append(remote(p_send.at[there], p_recv.at[y], pa_send.at[d, 0], pa_recv.at[d, 0], at_y(d)))
         p_out.append(remote(r_send.at[there], r_recv.at[y], pa_send.at[d, 1], pa_recv.at[d, 1], at_y(d)))
-    q_out = [remote(q_send, qb.at[h], qz_send.at[d], qz_recv.at[d], at_z(d)) for d in z_order]
+    q_out = [remote(q_send, qb.at[h], qz_send.at[d], qz_recv.at[d], at_z(d)) for d in z_near + z_far]
     w_out = []
     for step in range(2):
         for d in (1, 3):
             half = step if d == 1 else 1 - step
             rows = w.at[half_rows(0, c, half)]
             w_out.append(remote(rows, rows, wx_send.at[d, half], wx_recv.at[d, half], at_x(d)))
-    for copy in p_out + k_out + q_out + w_out:
+    for copy in p_out + k_out + q_out[:4] + w_out:
         copy.start()
     wc_out = []
 
@@ -173,6 +176,10 @@
 
     to_sibling(0, 0)
     to_sibling(0, 1)
+
+    pl.semaphore_wait(ready, 2)
+    for copy in q_out[4:]:
+        copy.start()
 
     for copy in k_out:
         copy.wait_recv()
@@ -383,10 +390,13 @@
             outs.append(out.reshape(32, 8, 128))
         o_send[pair] = jnp.concatenate(outs, axis=1).astype(BF)
 
-        @pl.loop(1, 32)
-        def _(d):
-            there = lax.rem(h + d, 32)
-            remote(o_send.at[pair, there], out_ref.at[h, pair], o_ssem.at[pair], o_rsem.at[pair], (g, there)).start()
+        for dz in z_order + (0,):
+            for dy in (2, 1, 3, 0):
+                if dy or dz:
+                    there = lax.rem(y + dy, NY) * NZ + lax.rem(z + dz, NZ)
+                    remote(
+                        o_send.at[pair, there], out_ref.at[h, pair], o_ssem.at[pair], o_rsem.at[pair], (g, there)
+                    ).start()
 
         keep = pltpu.make_async_copy(o_send.at[pair, h], out_ref.at[h, pair], local_sem.at[5 + pair])
         keep.start()
@@ -461,6 +471,7 @@
             *[dma((8,))] * 4,
             *[dma((4, 2))] * 2,
             *[dma((2,))] * 2,
+            pltpu.SemaphoreType.REGULAR,
         ],
         compiler_params=pltpu.CompilerParams(collective_id=0, has_side_effects=True, vmem_limit_bytes=60 << 20),
     )(

time: 43.4 us -> 42.5 us (0.979)
  Pallas kernels: 40.9 us -> 40.1 us
    pallas_call x1, Pallas kernels: 40.9 us -> 40.1 us  [local(): pl.pallas_call(kernel, out_shape=jax.ShapeDtypeStruct((32, 2, 16, 128), B...]
where the time goes in v4:
time: 42.5 us; the launch traced here: 42.4 us
  Pallas kernels  40.1 us (94%)
  local copies, waits for them, and re-layouts  1.67 us (4%)
  between operations  0.66 us (2%)
    pallas_call x1, Pallas kernels, local(): pl.pallas_call(kernel, out_shape=jax.ShapeDtypeStruct((32, 2, 16, 128), B...  40.1 us
    unnamed x1, local copies, waits for them, and re-layouts  1.67 us

profile of v4, /device:TPU:2, one launch (start us, length us, event | category | flops | bytes accessed | tf_op | source)
XLA Modules:
  0.0 42.4 jit_solution(8633186322825216337)
XLA Ops:
  0.7 40.1 %shard_map.100 = bf16[32,2,16,128]{3,2,1,0:T(8,128)(2,1)} custom-call(s32[1,1]{1,0:T(1,128)} %bitcast.6.owner_hbm, bf16[8,1536]{1,0:T(8,128)(2,1)} %query_hbm.1, bf16[8,576]{1,0:T(8,128)(2,1)} %keys_hbm.1, s32[1,16]{1,0:T(1,128)} %length_hbm.1, f32[32,256]{1,0:T(8,128)} %constant.2.clone.table_hbm, bf16[1,147456]{1,0:T(2,128)(2,1)} %prompt_hbm.1, ...), custom_call_target="tpu_custom_call" | custom-call | tf_op jit(solution)/shard_map/pallas_call | solution.py:421
  40.7 1.7 %copy.13 = bf16[8,16384]{1,0:T(8,128)(2,1)} copy(bf16[8,16384]{1,0:T(8,128)(2,1)} %bitcast.7) | data formatting | bytes 524288

commit v5 on v4

--- a/solution.py
+++ b/solution.py
@@ -126,7 +126,7 @@
     query = query_ref[...].astype(F32)
     packed = jnp.concatenate([query[:, :768], query[:, 768:]], axis=0).astype(BF)
     q_send[...] = packed
-    qb[pl.ds(h, 1)] = packed[None]
+    qb[pl.ds(y, 1), 4:5] = packed[None, None]
     keys_copy.wait()
     keys = keys_ref[...].astype(F32)
     packed = jnp.concatenate([keys[:, :256], keys[:, 256:512]], axis=0).astype(BF)
@@ -150,7 +150,7 @@
         k_out.append(remote(r_own, kt.at[y], ky_send.at[d, 1], ky_recv.at[d, 1], at_y(d)))
         p_out.append(remote(p_send.at[there], p_recv.at[y], pa_send.at[d, 0], pa_recv.at[d, 0], at_y(d)))
         p_out.append(remote(r_send.at[there], r_recv.at[y], pa_send.at[d, 1], pa_recv.at[d, 1], at_y(d)))
-    q_out = [remote(q_send, qb.at[h], qz_send.at[d], qz_recv.at[d], at_z(d)) for d in z_near + z_far]
+    q_out = [remote(q_send, qb.at[y, (12 - d) % NZ], qz_send.at[d], qz_recv.at[d], at_z(d)) for d in z_near + z_far]
     w_out = []
     for step in range(2):
         for d in (1, 3):
@@ -217,6 +217,16 @@
         wf_out.append(remote(rows, rows, wf_send.at[half], wf_recv.at[half], at_x(d)))
         wf_out[-1].start()
         to_sibling(NX - d, half)
+
+    def query_hop(ssem, rsem, n, dy, first, last, d):
+        part = qb.at[lax.rem(y + dy + NY, NY), first:last]
+        return remote(part, part, ssem.at[d, n], rsem.at[d, n], at_y(d))
+
+    for copy in q_out[:4]:
+        copy.wait_recv()
+    qy_near = [query_hop(qy_send, qy_recv, 0, 0, 2, 7, d) for d in (1, 3)]
+    for copy in qy_near:
+        copy.start()
 
     owner_copy.wait()
     owner = owner_ref[0, 0]
@@ -236,37 +246,34 @@
     pass_on(1, 0)
     pass_on(3, 1)
 
-    for copy in q_out:
-        copy.wait_recv()
-
-    def query_rows(dy, half):
-        return qb.at[pl.ds(lax.rem(y + dy + NY, NY) * NZ + half * 4, 4)]
-
-    qy_out, qf_out = [], []
-    for step in range(2):
-        for d in (1, 3):
-            half = step if d == 1 else 1 - step
-            part = query_rows(0, half)
-            qy_out.append(remote(part, part, qy_send.at[d, half], qy_recv.at[d, half], at_y(d)))
-    for copy in qy_out + kz_out:
+    for copy in q_out[4:]:
+        copy.wait_recv()
+    qy_far = [query_hop(qy_send, qy_recv, 1, 0, 0, 2, d) for d in (1, 3)]
+    qy_far += [query_hop(qy_send, qy_recv, 2, 0, 7, 8, d) for d in (3, 1)]
+    for copy in qy_far + kz_out:
+        copy.start()
+    for copy in qy_near:
+        copy.wait_recv()
+    qf_out = [query_hop(qf_send, qf_recv, 0, -1, 2, 5, 1), query_hop(qf_send, qf_recv, 0, 1, 5, 7, 3)]
+    for copy in qf_out:
         copy.start()
 
     for copy in pz_out:
         copy.wait_recv()
-    pl_buf[pl.ds(y, 1), pl.ds(z, 1)] = z_recv[owner % NZ][None, None]
-    pg_out = [remote(pl_buf.at[y, z], pl_buf.at[y, z], pg_send.at[d], pg_recv.at[d], at_z(d)) for d in z_order]
-    for copy in pg_out:
+    pl_buf[pl.ds(y, 1), 4:5] = z_recv[owner % NZ][None, None]
+    pg_out = {}
+    for d in z_order:
+        pg_out[d] = remote(pl_buf.at[y, 4], pl_buf.at[y, (12 - d) % NZ], pg_send.at[d], pg_recv.at[d], at_z(d))
+        pg_out[d].start()
+    for copy in qy_far:
+        copy.wait_recv()
+    qf_far = [query_hop(qf_send, qf_recv, 1, 1, 0, 2, 3), query_hop(qf_send, qf_recv, 1, -1, 7, 8, 1)]
+    for copy in qf_far:
         copy.start()
     for copy in kz_out:
         copy.wait_recv()
     for copy in kf_out:
         copy.start()
-    for n, (d, half) in enumerate(((1, 0), (3, 1))):
-        qy_out[n].wait_recv()
-        part = query_rows(-1 if d == 1 else 1, half)
-        qf_out.append(remote(part, part, qf_send.at[half], qf_recv.at[half], at_y(d)))
-        qf_out[-1].start()
-
     arrived(1, 1)
     to_sibling(3, 1)
     arrived(3, 0)
@@ -276,22 +283,31 @@
         remote(rows, rows, wf_send.at[half], wf_recv.at[half], sibling).wait_recv()
         to_sibling(2, half)
 
-    for copy in pg_out:
-        copy.wait_recv()
     py_out = []
-    for d in y_order:
-        part = pl_buf.at[y, :, :, 0:256]
-        py_out.append(remote(part, part, py_send.at[d, 0], py_recv.at[d, 0], at_y(d)))
-        part = pl_buf.at[y, 0:2, :, 256:384]
-        py_out.append(remote(part, part, py_send.at[d, 1], py_recv.at[d, 1], at_y(d)))
-    for copy in py_out:
-        copy.start()
-
-    for copy in qy_out[2:] + qf_out:
-        copy.wait_recv()
-    gathered = qb[...].astype(F32)
-    x_buf[:, :768] = gathered[:, :8].reshape(TOK, 768).astype(BF)
-    x_buf[:, 768:] = gathered[:, 8:].reshape(TOK, 768).astype(BF)
+
+    def spread_prompt(n, *index):
+        part = pl_buf.at[(y, *index)]
+        for d in y_order:
+            py_out.append(remote(part, part, py_send.at[d, n], py_recv.at[d, n], at_y(d)))
+            py_out[-1].start()
+
+    for d in z_near:
+        pg_out[d].wait_recv()
+    spread_prompt(0, slice(2, 7), slice(None), slice(0, 256))
+    spread_prompt(1, slice(4, 6), slice(None), slice(256, 384))
+    for d in z_far:
+        pg_out[d].wait_recv()
+    spread_prompt(2, slice(0, 2), slice(None), slice(0, 256))
+    spread_prompt(3, slice(7, 8), slice(None), slice(0, 256))
+
+    for copy in qf_out + qf_far:
+        copy.wait_recv()
+    for j in range(NY):
+        gathered = jnp.concatenate(
+            [qb[pl.ds(j, 1), pl.ds(lax.rem(k - z + 12, NZ), 1)].astype(F32)[0] for k in range(NZ)], axis=0
+        )
+        x_buf[j * 64 : (j + 1) * 64, :768] = gathered[:, :8].reshape(64, 768).astype(BF)
+        x_buf[j * 64 : (j + 1) * 64, 768:] = gathered[:, 8:].reshape(64, 768).astype(BF)
     for dx in range(NX):
         for half in range(2):
             from_sibling(dx, half)
@@ -354,10 +370,21 @@
     gathered = pl_buf[:, :, :, :256].astype(F32).reshape(32, 16, 256)
     latent[:, :256] = gathered[:, :8].reshape(PLEN, 256).astype(BF)
     latent[:, 256:] = gathered[:, 8:].reshape(PLEN, 256).astype(BF)
+    tiles = []
     for j in range(NY):
-        both = jnp.concatenate([pl_buf[j, 0, :, 256:], pl_buf[j, 1, :, 256:]], axis=1)
-        rotary[j * 16 : (j + 1) * 16, :] = both
-        rotary[64 + j * 16 : 64 + (j + 1) * 16, :] = both
+        tiles.append(
+            jnp.concatenate(
+                [pl_buf[pl.ds(j, 1), pl.ds(4 + lax.rem(z + n, 2), 1), :, 256:].astype(F32)[0, 0] for n in range(2)], axis=1
+            )
+        )
+    tiles = jnp.concatenate(tiles, axis=0)
+    turn = lax.rem(z + 4, NZ) * 8
+    key_lane = lax.broadcasted_iota(jnp.int32, (ROPE, PLEN), 1) % 64
+    tiles = jnp.where(
+        key_lane < 64 - turn, pltpu.roll(tiles, lax.rem(PLEN - turn, PLEN), 1), pltpu.roll(tiles, 64 - turn, 1)
+    ).astype(BF)
+    rotary[:64, :] = tiles
+    rotary[64:, :] = tiles
 
     for pair in range(2):
         outs = []
@@ -401,7 +428,7 @@
         keep = pltpu.make_async_copy(o_send.at[pair, h], out_ref.at[h, pair], local_sem.at[5 + pair])
         keep.start()
 
-    for copy in w_out + wf_out + wc_out + k_out + q_out + qy_out + qf_out + kz_out + kf_out + p_out + pz_out + pg_out + py_out:
+    for copy in w_out + wf_out + wc_out + k_out + q_out + qy_near + qy_far + qf_out + qf_far + kz_out + kf_out + p_out + pz_out + list(pg_out.values()) + py_out:
         copy.wait_send()
     for pair in range(2):
         pltpu.make_async_copy(o_send.at[pair, h], out_ref.at[h, pair], local_sem.at[5 + pair]).wait()
@@ -437,7 +464,7 @@
             pltpu.VMEM((16, 768), BF),
             pltpu.VMEM((16, 256), BF),
             pltpu.VMEM((16, 128), BF),
-            pltpu.VMEM((32, 16, 768), BF),
+            pltpu.VMEM((NY, NZ, 16, 768), BF),
             pltpu.VMEM((NY, NZ, 16, 256), BF),
             pltpu.VMEM((NY, 16, 128), BF),
             pltpu.VMEM((NZ, 16, 128), BF),
@@ -463,13 +490,13 @@
             *[dma((2,))] * 2,
             *[dma((4, 2))] * 2,
             *[dma((8,))] * 2,
+            *[dma((4, 3))] * 2,
             *[dma((4, 2))] * 2,
-            *[dma((2,))] * 2,
             *[dma((4, 2))] * 2,
             *[dma((8, 2))] * 2,
             *[dma((4, 2))] * 2,
             *[dma((8,))] * 4,
-            *[dma((4, 2))] * 2,
+            *[dma((4, 4))] * 2,
             *[dma((2,))] * 2,
             pltpu.SemaphoreType.REGULAR,
         ],

time: 42.5 us -> 42.1 us (level)
  Pallas kernels: 40.1 us -> 39.6 us
    pallas_call x1, Pallas kernels: 40.1 us -> 39.6 us  [local(): pl.pallas_call(kernel, out_shape=jax.ShapeDtypeStruct((32, 2, 16, 128), B...]
where the time goes in v5:
time: 42.1 us; the launch traced here: 41.9 us
  Pallas kernels  39.6 us (94%)
  local copies, waits for them, and re-layouts  1.67 us (4%)
  between operations  0.66 us (2%)
    pallas_call x1, Pallas kernels, local(): pl.pallas_call(kernel, out_shape=jax.ShapeDtypeStruct((32, 2, 16, 128), B...  39.6 us
    unnamed x1, local copies, waits for them, and re-layouts  1.67 us

profile of v5, /device:TPU:2, one launch (start us, length us, event | category | flops | bytes accessed | tf_op | source)
XLA Modules:
  0.0 41.9 jit_solution(1167650647508791463)
XLA Ops:
  0.7 39.6 %shard_map.100 = bf16[32,2,16,128]{3,2,1,0:T(8,128)(2,1)} custom-call(s32[1,1]{1,0:T(1,128)} %bitcast.6.owner_hbm, bf16[8,1536]{1,0:T(8,128)(2,1)} %query_hbm.1, bf16[8,576]{1,0:T(8,128)(2,1)} %keys_hbm.1, s32[1,16]{1,0:T(1,128)} %length_hbm.1, f32[32,256]{1,0:T(8,128)} %constant.2.clone.table_hbm, bf16[1,147456]{1,0:T(2,128)(2,1)} %prompt_hbm.1, ...), custom_call_target="tpu_custom_call" | custom-call | tf_op jit(solution)/shard_map/pallas_call | solution.py:448
  40.3 1.7 %copy.13 = bf16[8,16384]{1,0:T(8,128)(2,1)} copy(bf16[8,16384]{1,0:T(8,128)(2,1)} %bitcast.7) | data formatting | bytes 524288

commit v6 on v5

--- a/solution.py
+++ b/solution.py
@@ -357,12 +357,12 @@
         part = turned[:, (i // 2) * 128 : (i // 2 + 1) * 128].astype(F32)
         return jnp.where(mine_lanes, part, 0.0).astype(BF)
 
-    for i in range(4):
-        t = own_turned(i)
-        for half in range(2):
-            part = slice(half * 128, (half + 1) * 128)
-            scores = dot_nt(absorbed[i, part, :], fresh[part, :]) + dot_nt(t[part], fresh_rot[part, :])
-            own_buf[i, part, :] = jnp.where(allowed, scores, -jnp.inf)
+    for half in range(2):
+        part = slice(half * 128, (half + 1) * 128)
+        a = absorbed[:, part, :].reshape(512, LAT)
+        t = jnp.concatenate([own_turned(i)[part] for i in range(4)], axis=0)
+        scores = dot_nt(a, fresh[part, :]) + dot_nt(t, fresh_rot[part, :])
+        own_buf[:, part, :] = jnp.where(allowed[None], scores.reshape(4, 128, 128), -jnp.inf)
     vu_copy.wait()
 
     for copy in py_out:
@@ -386,34 +386,39 @@
     rotary[:64, :] = tiles
     rotary[64:, :] = tiles
 
+    latent_t = latent[...].T
     for pair in range(2):
+        a = absorbed[pair * 2 : pair * 2 + 2].reshape(512, LAT)
+        t = jnp.concatenate([own_turned(pair * 2), own_turned(pair * 2 + 1)], axis=0)
+        prompt_scores = jnp.dot(a, latent_t, preferred_element_type=F32) + jnp.dot(t, rotary[...], preferred_element_type=F32)
+        own_scores = own_buf[pair * 2 : pair * 2 + 2].reshape(512, 128)
+        top = jnp.max(
+            jnp.maximum(jnp.maximum(prompt_scores[:, :128], prompt_scores[:, 128:]), own_scores), axis=1, keepdims=True
+        )
+        prompt_exp = jnp.exp2((prompt_scores - top) * (SCALE * LOG2E))
+        own_exp = jnp.exp2((own_scores - top) * (SCALE * LOG2E))
+        total = jnp.sum(prompt_exp[:, :128] + prompt_exp[:, 128:] + own_exp, axis=1, keepdims=True)
+        factor = jnp.where(jnp.concatenate([live, live], axis=0), 1.0 / total, 0.0)
+        mixed = jnp.dot(prompt_exp.astype(BF), latent[...], preferred_element_type=F32)
+        own_weight = own_exp.reshape(2, 2, 128, 128)
+        mixed_own = jnp.concatenate(
+            [
+                jnp.dot(
+                    own_weight[:, half].reshape(256, 128).astype(BF),
+                    fresh[half * 128 : (half + 1) * 128, :],
+                    preferred_element_type=F32,
+                ).reshape(2, 128, LAT)
+                for half in range(2)
+            ],
+            axis=1,
+        ).reshape(512, LAT)
+        mixed = ((mixed + mixed_own) * factor).astype(BF)
         outs = []
         for sub in range(2):
             i = pair * 2 + sub
-            prompt_scores = dot_nt(absorbed[i], latent[...]) + jnp.dot(
-                own_turned(i), rotary[...], preferred_element_type=F32
+            out = jnp.dot(
+                mixed[sub * TOK : (sub + 1) * TOK], vu[:, i * 128 : (i + 1) * 128], preferred_element_type=F32
             )
-            own_scores = own_buf[i]
-            top = jnp.max(
-                jnp.maximum(jnp.maximum(prompt_scores[:, :128], prompt_scores[:, 128:]), own_scores),
-                axis=1,
-                keepdims=True,
-            )
-            prompt_exp = jnp.exp2((prompt_scores - top) * (SCALE * LOG2E))
-            own_exp = jnp.exp2((own_scores - top) * (SCALE * LOG2E))
-            total = jnp.sum(prompt_exp[:, :128] + prompt_exp[:, 128:] + own_exp, axis=1, keepdims=True)
-            factor = jnp.where(live, 1.0 / total, 0.0)
-            own_weight = own_exp.astype(BF)
-            mixed = jnp.dot(prompt_exp.astype(BF), latent[...], preferred_element_type=F32)
-            mixed_own = jnp.concatenate(
-                [
-                    jnp.dot(own_weight[:128], fresh[:128, :], preferred_element_type=F32),
-                    jnp.dot(own_weight[128:], fresh[128:, :], preferred_element_type=F32),
-                ],
-                axis=0,
-            )
-            mixed = ((mixed + mixed_own) * factor).astype(BF)
-            out = jnp.dot(mixed, vu[:, i * 128 : (i + 1) * 128], preferred_element_type=F32)
             outs.append(out.reshape(32, 8, 128))
         o_send[pair] = jnp.concatenate(outs, axis=1).astype(BF)
 

time: 42.1 us -> 41.9 us (level)
  no operation moved by 1% of the time
where the time goes in v6:
time: 41.9 us; the launch traced here: 41.8 us
  Pallas kernels  39.5 us (94%)
  local copies, waits for them, and re-layouts  1.67 us (4%)
  between operations  0.66 us (2%)
    pallas_call x1, Pallas kernels, local(): pl.pallas_call(kernel, out_shape=jax.ShapeDtypeStruct((32, 2, 16, 128), B...  39.5 us
    unnamed x1, local copies, waits for them, and re-layouts  1.67 us

profile of v6, /device:TPU:2, one launch (start us, length us, event | category | flops | bytes accessed | tf_op | source)
XLA Modules:
  0.0 41.8 jit_solution(12618064100434917742)
XLA Ops:
  0.7 39.5 %shard_map.100 = bf16[32,2,16,128]{3,2,1,0:T(8,128)(2,1)} custom-call(s32[1,1]{1,0:T(1,128)} %bitcast.6.owner_hbm, bf16[8,1536]{1,0:T(8,128)(2,1)} %query_hbm.1, bf16[8,576]{1,0:T(8,128)(2,1)} %keys_hbm.1, s32[1,16]{1,0:T(1,128)} %length_hbm.1, f32[32,256]{1,0:T(8,128)} %constant.2.clone.table_hbm, bf16[1,147456]{1,0:T(2,128)(2,1)} %prompt_hbm.1, ...), custom_call_target="tpu_custom_call" | custom-call | tf_op jit(solution)/shard_map/pallas_call | solution.py:453
  40.1 1.7 %copy.13 = bf16[8,16384]{1,0:T(8,128)(2,1)} copy(bf16[8,16384]{1,0:T(8,128)(2,1)} %bitcast.7) | data formatting | bytes 524288

commit v7 on v6

--- a/solution.py
+++ b/solution.py
@@ -126,7 +126,7 @@
     query = query_ref[...].astype(F32)
     packed = jnp.concatenate([query[:, :768], query[:, 768:]], axis=0).astype(BF)
     q_send[...] = packed
-    qb[pl.ds(y, 1), 4:5] = packed[None, None]
+    qb[pl.ds(y, 1), 2:3] = packed[None, None]
     keys_copy.wait()
     keys = keys_ref[...].astype(F32)
     packed = jnp.concatenate([keys[:, :256], keys[:, 256:512]], axis=0).astype(BF)
@@ -150,7 +150,7 @@
         k_out.append(remote(r_own, kt.at[y], ky_send.at[d, 1], ky_recv.at[d, 1], at_y(d)))
         p_out.append(remote(p_send.at[there], p_recv.at[y], pa_send.at[d, 0], pa_recv.at[d, 0], at_y(d)))
         p_out.append(remote(r_send.at[there], r_recv.at[y], pa_send.at[d, 1], pa_recv.at[d, 1], at_y(d)))
-    q_out = [remote(q_send, qb.at[y, (12 - d) % NZ], qz_send.at[d], qz_recv.at[d], at_z(d)) for d in z_near + z_far]
+    q_out = [remote(q_send, qb.at[y, (10 - d) % NZ], qz_send.at[d], qz_recv.at[d], at_z(d)) for d in z_near + z_far]
     w_out = []
     for step in range(2):
         for d in (1, 3):
@@ -224,7 +224,7 @@
 
     for copy in q_out[:4]:
         copy.wait_recv()
-    qy_near = [query_hop(qy_send, qy_recv, 0, 0, 2, 7, d) for d in (1, 3)]
+    qy_near = [query_hop(qy_send, qy_recv, 0, 0, 0, 5, d) for d in (1, 3)]
     for copy in qy_near:
         copy.start()
 
@@ -248,26 +248,25 @@
 
     for copy in q_out[4:]:
         copy.wait_recv()
-    qy_far = [query_hop(qy_send, qy_recv, 1, 0, 0, 2, d) for d in (1, 3)]
-    qy_far += [query_hop(qy_send, qy_recv, 2, 0, 7, 8, d) for d in (3, 1)]
+    qy_far = [query_hop(qy_send, qy_recv, 1, 0, 5, 8, d) for d in (1, 3)]
     for copy in qy_far + kz_out:
         copy.start()
     for copy in qy_near:
         copy.wait_recv()
-    qf_out = [query_hop(qf_send, qf_recv, 0, -1, 2, 5, 1), query_hop(qf_send, qf_recv, 0, 1, 5, 7, 3)]
+    qf_out = [query_hop(qf_send, qf_recv, 0, -1, 0, 3, 1), query_hop(qf_send, qf_recv, 0, 1, 3, 5, 3)]
     for copy in qf_out:
         copy.start()
 
     for copy in pz_out:
         copy.wait_recv()
-    pl_buf[pl.ds(y, 1), 4:5] = z_recv[owner % NZ][None, None]
+    pl_buf[pl.ds(y, 1), 2:3] = z_recv[owner % NZ][None, None]
     pg_out = {}
     for d in z_order:
-        pg_out[d] = remote(pl_buf.at[y, 4], pl_buf.at[y, (12 - d) % NZ], pg_send.at[d], pg_recv.at[d], at_z(d))
+        pg_out[d] = remote(pl_buf.at[y, 2], pl_buf.at[y, (10 - d) % NZ], pg_send.at[d], pg_recv.at[d], at_z(d))
         pg_out[d].start()
     for copy in qy_far:
         copy.wait_recv()
-    qf_far = [query_hop(qf_send, qf_recv, 1, 1, 0, 2, 3), query_hop(qf_send, qf_recv, 1, -1, 7, 8, 1)]
+    qf_far = [query_hop(qf_send, qf_recv, 1, 1, 6, 8, 3), query_hop(qf_send, qf_recv, 1, -1, 5, 6, 1)]
     for copy in qf_far:
         copy.start()
     for copy in kz_out:
@@ -293,18 +292,17 @@
 
     for d in z_near:
         pg_out[d].wait_recv()
-    spread_prompt(0, slice(2, 7), slice(None), slice(0, 256))
-    spread_prompt(1, slice(4, 6), slice(None), slice(256, 384))
+    spread_prompt(0, slice(0, 5), slice(None), slice(0, 256))
+    spread_prompt(1, slice(2, 4), slice(None), slice(256, 384))
     for d in z_far:
         pg_out[d].wait_recv()
-    spread_prompt(2, slice(0, 2), slice(None), slice(0, 256))
-    spread_prompt(3, slice(7, 8), slice(None), slice(0, 256))
+    spread_prompt(2, slice(5, 8), slice(None), slice(0, 256))
 
     for copy in qf_out + qf_far:
         copy.wait_recv()
     for j in range(NY):
         gathered = jnp.concatenate(
-            [qb[pl.ds(j, 1), pl.ds(lax.rem(k - z + 12, NZ), 1)].astype(F32)[0] for k in range(NZ)], axis=0
+            [qb[pl.ds(j, 1), pl.ds(lax.rem(k - z + 10, NZ), 1)].astype(F32)[0] for k in range(NZ)], axis=0
         )
         x_buf[j * 64 : (j + 1) * 64, :768] = gathered[:, :8].reshape(64, 768).astype(BF)
         x_buf[j * 64 : (j + 1) * 64, 768:] = gathered[:, 8:].reshape(64, 768).astype(BF)
@@ -374,11 +372,11 @@
     for j in range(NY):
         tiles.append(
             jnp.concatenate(
-                [pl_buf[pl.ds(j, 1), pl.ds(4 + lax.rem(z + n, 2), 1), :, 256:].astype(F32)[0, 0] for n in range(2)], axis=1
+                [pl_buf[pl.ds(j, 1), pl.ds(2 + lax.rem(z + n, 2), 1), :, 256:].astype(F32)[0, 0] for n in range(2)], axis=1
             )
         )
     tiles = jnp.concatenate(tiles, axis=0)
-    turn = lax.rem(z + 4, NZ) * 8
+    turn = lax.rem(z + 6, NZ) * 8
     key_lane = lax.broadcasted_iota(jnp.int32, (ROPE, PLEN), 1) % 64
     tiles = jnp.where(
         key_lane < 64 - turn, pltpu.roll(tiles, lax.rem(PLEN - turn, PLEN), 1), pltpu.roll(tiles, 64 - turn, 1)

time: 41.9 us -> 41.9 us (level)
  no operation moved by 1% of the time
where the time goes in v7:
time: 41.9 us; the launch traced here: 41.8 us
  Pallas kernels  39.4 us (94%)
  local copies, waits for them, and re-layouts  1.67 us (4%)
  between operations  0.66 us (2%)
    pallas_call x1, Pallas kernels, local(): pl.pallas_call(kernel, out_shape=jax.ShapeDtypeStruct((32, 2, 16, 128), B...  39.4 us
    unnamed x1, local copies, waits for them, and re-layouts  1.67 us

profile of v7, /device:TPU:2, one launch (start us, length us, event | category | flops | bytes accessed | tf_op | source)
XLA Modules:
  0.0 41.8 jit_solution(6014272920924926835)
XLA Ops:
  0.7 39.4 %shard_map.100 = bf16[32,2,16,128]{3,2,1,0:T(8,128)(2,1)} custom-call(s32[1,1]{1,0:T(1,128)} %bitcast.6.owner_hbm, bf16[8,1536]{1,0:T(8,128)(2,1)} %query_hbm.1, bf16[8,576]{1,0:T(8,128)(2,1)} %keys_hbm.1, s32[1,16]{1,0:T(1,128)} %length_hbm.1, f32[32,256]{1,0:T(8,128)} %constant.2.clone.table_hbm, bf16[1,147456]{1,0:T(2,128)(2,1)} %prompt_hbm.1, ...), custom_call_target="tpu_custom_call" | custom-call | tf_op jit(solution)/shard_map/pallas_call | solution.py:451
  40.1 1.7 %copy.13 = bf16[8,16384]{1,0:T(8,128)(2,1)} copy(bf16[8,16384]{1,0:T(8,128)(2,1)} %bitcast.7) | data formatting | bytes 524288
